TPU v7x, 256 devices: a whole 4x4x8 slice. The times are simulated.
256 devices in a mesh: dp: 32 (over z_hi, x, core), fsdp: 8 (over y, z_lo).
Axes of the slice: x: 4, y: 4, z: 8 (z_hi: 4, z_lo: 2; z = z_hi * 2 + z_lo), core: 2. Of those that a mesh axis runs over, the one named last changes fastest.
Arguments:
- frames_in: bfloat16 [98304, 1536], P(('dp', 'fsdp')), may hold values from -6 to 6
- dest: int32 [98304], P(('dp', 'fsdp')), may hold values from 0 to 3071, as said below
- segment: int32 [32, 3072], P('dp', 'fsdp'), may hold values from 0 to 11, never falling along the last dimension, each value on 1 to 576 neighbouring positions
- gain_in: float32 [1536], replicated, may hold values from 0.5 to 1.5
- w_glu: bfloat16 [1536, 3072], P('fsdp'), may hold values from -0.15625 to 0.15625
- kernel: float32 [31, 1536], replicated, may hold values from -1 to 1
- gain_mid: float32 [1536], replicated, may hold values from 0.5 to 1.5
- cotangent: bfloat16 [98304, 1536], P(('dp', 'fsdp')), may hold values from -6 to 6
Outputs:
- output: bfloat16 [98304, 1536], P(('dp', 'fsdp'))
- grad_frames: bfloat16 [98304, 1536], P(('dp', 'fsdp'))
- grad_weight: float32 [1536, 3072], P('fsdp')
- grad_gain_in: float32 [1536], replicated
- grad_kernel: float32 [31, 1536], replicated
- grad_gain_mid: float32 [1536], replicated
Inputs may be any that keep to these rules, and one draw needn't show every extreme that they name: Within each dp index's 3072 rows, dest is a permutation of 0 to 3071, and the 384 rows of each device name exactly 48 positions in each range of 384 positions k * 384 to (k + 1) * 384 - 1.
All inputs are finite; a program needn't handle non-finite values.
Results may differ from a plain program's by a relative error of at most 0.0065.
Values may be sent and summed in bfloat16 or wider, within the bound.
A program may use at most 128 MiB of HBM per device.

v0:
```python
import jax
import jax.numpy as jnp
from jax import lax
from jax.sharding import PartitionSpec as P

EPS = 1e-05


def padded(cells, sides, width):
    for axis, dim in sides:
        count = lax.axis_size(axis)
        ends = count - 1
        head = lax.slice_in_dim(cells, 0, width, axis=dim)
        tail = lax.slice_in_dim(cells, cells.shape[dim] - width, cells.shape[dim], axis=dim)
        cells = jnp.concatenate(
            [
                lax.ppermute(tail, axis, [(i, (i + 1) % count) for i in range(ends)]),
                cells,
                lax.ppermute(head, axis, [((i + 1) % count, i) for i in range(ends)]),
            ],
            axis=dim,
        )
    return cells


def norm_rows(values):
    centre = values - jnp.mean(values, axis=-1, keepdims=True)
    scale = lax.rsqrt(jnp.mean(centre * centre, axis=-1, keepdims=True) + EPS)
    return (centre * scale, scale)


def norm_back(upstream, unit, scale):
    return scale * (
        upstream
        - jnp.mean(upstream, axis=-1, keepdims=True)
        - unit * jnp.mean(upstream * unit, axis=-1, keepdims=True)
    )


def tap_masks(seg_ext, seg_own, taps):
    width = seg_own.shape[0]
    return jnp.stack([seg_ext[j : j + width] == seg_own for j in range(taps)], axis=1).astype(
        jnp.float32
    )


def depthwise(extended, masks, kernel):
    width = masks.shape[0]
    total = jnp.zeros((width, extended.shape[1]), jnp.float32)
    for j in range(kernel.shape[0]):
        total = (
            total + extended[j : j + width].astype(jnp.float32) * masks[:, j : j + 1] * kernel[j]
        )
    return total


def kernel_grad(extended, masks, upstream):
    width = masks.shape[0]
    return jnp.stack(
        [
            jnp.sum(
                upstream * extended[j : j + width].astype(jnp.float32) * masks[:, j : j + 1], axis=0
            )
            for j in range(masks.shape[1])
        ],
        axis=0,
    )


def on_device(frames_in, dest, segment, gain_in, w_glu, kernel, gain_mid, cotangent):
    groups = lax.axis_size("fsdp")
    rows, width = frames_in.shape
    block = rows // groups
    here = lax.axis_index("fsdp")
    taps = kernel.shape[0]
    half = (taps - 1) // 2
    order = jnp.argsort(dest, stable=True)
    outgoing = frames_in[order].reshape(groups, block, width)
    incoming = lax.all_to_all(outgoing, "fsdp", split_axis=0, concat_axis=0, tiled=True)
    every_dest = lax.all_gather(dest, "fsdp", axis=0, tiled=True).reshape(groups, rows)
    ordered = jnp.sort(every_dest, axis=1)
    mine = lax.dynamic_slice_in_dim(ordered, here * block, block, 1)
    slots = (mine - here * rows).reshape(-1)
    packed = jnp.zeros((rows, width), jnp.bfloat16).at[slots].set(incoming.reshape(rows, width))
    seg = segment[0]
    seg_ext = padded(seg, (("fsdp", 0),), half)
    masks = tap_masks(seg_ext, seg, taps)
    unit_in, scale_in = norm_rows(packed.astype(jnp.float32))
    normed = (unit_in * gain_in).astype(jnp.bfloat16)
    proj = jnp.dot(
        normed,
        lax.all_gather(w_glu, "fsdp", axis=0, tiled=True),
        preferred_element_type=jnp.float32,
    )
    value = proj[:, :width]
    sig = jax.nn.sigmoid(proj[:, width:])
    glu = (value * sig).astype(jnp.bfloat16)
    glu_ext = padded(glu, (("fsdp", 0),), half)
    mixed = depthwise(glu_ext, masks, kernel)
    unit_mid, scale_mid = norm_rows(mixed)
    mid = unit_mid * gain_mid
    sig_mid = jax.nn.sigmoid(mid)
    output = (packed.astype(jnp.float32) + mid * sig_mid).astype(jnp.bfloat16)
    cot_full = cotangent.astype(jnp.float32)
    d_mid = cot_full * (sig_mid + mid * sig_mid * (1.0 - sig_mid))
    g_gain_mid = jnp.sum(d_mid * unit_mid, axis=0)
    d_mixed = norm_back(d_mid * gain_mid, unit_mid, scale_mid)
    dm_ext = padded(d_mixed, (("fsdp", 0),), half)
    d_glu = depthwise(dm_ext, masks, kernel[::-1])
    g_kernel = kernel_grad(glu_ext, masks, d_mixed)
    d_proj = jnp.concatenate([d_glu * sig, d_glu * value * sig * (1.0 - sig)], axis=1).astype(
        jnp.bfloat16
    )
    replica_shard = lax.psum_scatter(
        jnp.dot(normed.T, d_proj, preferred_element_type=jnp.float32),
        "fsdp",
        scatter_dimension=0,
        tiled=True,
    )
    grad_weight = lax.psum(replica_shard, "dp")
    d_normed = jnp.dot(
        d_proj,
        lax.all_gather(w_glu, "fsdp", axis=0, tiled=True).T,
        preferred_element_type=jnp.float32,
    )
    g_gain_in = jnp.sum(d_normed * unit_in, axis=0)
    grad_frames = (cot_full + norm_back(d_normed * gain_in, unit_in, scale_in)).astype(jnp.bfloat16)
    grad_gain_in, grad_kernel, grad_gain_mid = lax.psum(
        (g_gain_in, g_kernel, g_gain_mid), ("dp", "fsdp")
    )
    return (output, grad_frames, grad_weight, grad_gain_in, grad_kernel, grad_gain_mid)


def solution(mesh):
    return jax.shard_map(
        on_device,
        mesh=mesh,
        in_specs=(
            P(("dp", "fsdp"), None),
            P(("dp", "fsdp")),
            P("dp", "fsdp"),
            P(),
            P("fsdp", None),
            P(),
            P(),
            P(("dp", "fsdp"), None),
        ),
        out_specs=(
            P(("dp", "fsdp"), None),
            P(("dp", "fsdp"), None),
            P("fsdp", None),
            P(),
            P(),
            P(),
        ),
        check_vma=False,
    )
```

profile of v0, /device:TPU:1, one launch (start us, length us, event | category | flops | bytes accessed | tf_op | source)
XLA Modules:
  0.0 1205.5 jit_solution(15038350292448875277)
XLA Ops:
  8.1 0.8 reshape.117
  8.8 20.3 %all-gather = s32[8,1,384]{2,1,0:T(1,128)S(1)} all-gather(s32[1,1,384]{2,1,0:T(1,128)S(1)} %reshape.117), channel_id=1, replica_groups=mesh['dp'=32,'fsdp'=8] {'fsdp'}, dimensions={0}, use_global_device_ids=true | all-gather | bytes 13824 | tf_op jit(solution)/shard_map/all_gather | solution.py:80
  30.4 4.4 sort.26
  34.8 2.8 gather_fusion
  37.7 4.1 all-to-all-start
  41.9 1.3 collective-permute-start.2
  43.2 4.0 collective-permute-start.1
  48.1 3.3 collective-permute-done.2
  52.1 0.7 slice_reduce_fusion.61
  52.9 0.8 dynamic-slice_subtract_fusion
  53.8 2.7 scatter_custom_fusion
  57.2 178.1 %all-gather.3.cloned.1.call-done = bf16[1536,3072]{1,0:T(8,128)(2,1)} async-done(((bf16[192,3072]{1,0:T(8,128)(2,1)}), bf16[1536,3072]{1,0:T(8,128)(2,1)}) %all-gather.3.cloned.1.call-update) | async-done | bytes 9437200 | tf_op jit(solution)/shard_map/all_gather | solution.py:92
  235.3 6.7 fusion.294
  242.6 3.0 collective-permute-start
  245.6 1.8 collective-permute-start.3
  248.1 2.4 collective-permute-done.3
  250.8 24.5 %fusion.297 = (f32[384]{0:T(512)S(1)}, f32[384,1536]{1,0:T(8,128)S(1)}) fusion(f32[1536]{0:T(1024)S(1)} %get-tuple-element.74, f32[384]{0:T(512)} %get-tuple-element.77, bf16[15,1536]{1,0:T(8,128)(2,1)S(1)} %collective-permute-done.3, bf16[384,1536]{1,0:T(8,128)(2,1)S(1)} %multiply_convert_fusion.2, f32[1536]{0:T(1024)S(1)} %get-tuple-element.75, ...), kind=kLoop, calls=%fused_computation.570 | loop fusion | flops 126221952 | bytes 3870720 | tf_op jit(solution)/shard_map/reduce_sum | solution.py:27
  275.8 3.6 multiply_reduce_fusion
  279.7 8.3 fusion.134
  288.0 4.1 collective-permute-start.4
  292.1 1.5 collective-permute-start.5
  293.8 4.1 collective-permute-done.5
  298.2 23.8 %multiply_convert_fusion.1 = (bf16[384,1536]{1,0:T(8,128)(2,1)}, f32[384,1536]{1,0:T(8,128)S(1)}) fusion(f32[384,3072]{1,0:T(8,128)S(1)} %fusion.294, f32[1536]{0:T(1024)S(1)} %copy-done.18, f32[384]{0:T(512)} %get-tuple-element.77, f32[15,1536]{1,0:T(8,128)S(1)} %collective-permute-done.5, f32[384,1536]{1,0:T(8,128)S(1)} %get-tuple-element.109, ...), kind=kLoop, calls=%fused_computation.413 | loop fusion | flops 74907648 | bytes 8679936 | tf_op jit(solution)/shard_map/convert
  322.1 0.9 multiply_convert_fusion
  323.0 1.0 copy-done.9
  324.1 9.4 fusion.258
  333.8 1.3 stack.254
  335.1 1.3 stack.252
  336.4 1.3 stack.251
  337.7 1.3 stack.250
  339.0 1.3 stack.249
  340.3 1.3 stack.248
  341.6 2.5 fusion.44
  345.9 3.6 fusion.92
  350.1 7.7 fusion.131
  363.2 4.1 fusion.80
  367.9 4.9 fusion.62
  373.0 5.9 stack.255
  379.0 326.4 %reduce-scatter.2.cloned.1.call-done = f32[192,3072]{1,0:T(8,128)} async-done(((f32[1536,3072]{1,0:T(8,128)}), f32[192,3072]{1,0:T(8,128)}) %reduce-scatter.2.cloned.1.call-update) | async-done | bytes 2359312 | tf_op jit(solution)/shard_map/reduce_scatter | solution.py:114
  705.5 10.3 fusion.10
  715.8 78.8 %all-reduce = (f32[1536]{0:T(1024)}, f32[1536]{0:T(1024)}) all-reduce(f32[1536]{0:T(1024)} %get-tuple-element.40, f32[1536]{0:T(1024)} %get-tuple-element.8), channel_id=1, replica_groups=mesh['dp'=32,'fsdp'=8] {'dp','fsdp'}, use_global_device_ids=true, to_apply=%region_14.15 | all-reduce | flops 3072 | bytes 24576 | tf_op jit(solution)/shard_map/psum | solution.py:128
  794.6 0.7 broadcast_multiply_fusion
  795.3 0.7 broadcast_multiply_fusion.1
  796.0 3.7 fusion.135
  799.7 99.8 %all-reduce.6.cloned.1.call-done = f32[31,1536]{1,0:T(8,128)} async-done(((f32[31,1536]{1,0:T(8,128)}), f32[31,1536]{1,0:T(8,128)}) %all-reduce.6.cloned.1.call-update) | async-done | bytes 190480 | tf_op jit(solution)/shard_map/psum | solution.py:128
  899.5 294.5 %all-reduce.4.cloned.1.call-done = f32[192,3072]{1,0:T(8,128)} async-done(((f32[192,3072]{1,0:T(8,128)}), f32[192,3072]{1,0:T(8,128)}) %all-reduce.4.cloned.1.call-update) | async-done | bytes 2359312 | tf_op jit(solution)/shard_map/psum | solution.py:120
  1194.0 3.4 copy.19
  1197.4 0.7 copy.20
  (289 shorter events, 14.4 us)
Async XLA Ops:
  29.8 205.5 %all-gather.3.cloned.1.call-start = ((), (), s32[]{:S(2)}) async-start(), calls=%async_computation.2 | async-start | bytes 10616832 | tf_op jit(solution)/shard_map/all_gather | solution.py:92
  37.7 16.1 %all-to-all-start = ((bf16[8,48,1536]{2,1,0:T(8,128)(2,1)}), bf16[8,48,1536]{2,1,0:T(8,128)(2,1)S(1)}, u32[]{:S(2)}, u32[]{:S(2)}) async-start(bf16[8,48,1536]{2,1,0:T(8,128)(2,1)} %bitcast), calls=%async_computation | async-start | bytes 2359296 | tf_op jit(solution)/shard_map/all_to_all | solution.py:79
  41.8 663.7 %reduce-scatter.2.cloned.1.call-start = ((), (), s32[]{:S(2)}) async-start(), calls=%async_computation.3 | async-start | bytes 21233664 | tf_op jit(solution)/shard_map/reduce_scatter | solution.py:114
  41.9 9.4 collective-permute-start.2
  43.2 8.1 collective-permute-start.1
  47.4 203.0 %copy-start.55 = (f32[1536]{0:T(1024)}, f32[1536]{0:T(1024)S(1)}, u32[]{:S(2)}) copy-start(f32[1536]{0:T(1024)S(1)} %get-tuple-element.64) | copy-start | bytes 18436
  47.4 203.0 %copy-start.57 = (f32[1536]{0:T(1024)}, f32[1536]{0:T(1024)S(1)}, u32[]{:S(2)}) copy-start(f32[1536]{0:T(1024)S(1)} %get-tuple-element.65) | copy-start | bytes 18436
  47.4 203.0 %copy-start.59 = (f32[1536]{0:T(1024)}, f32[1536]{0:T(1024)S(1)}, u32[]{:S(2)}) copy-start(f32[1536]{0:T(1024)S(1)} %get-tuple-element.66) | copy-start | bytes 18436
  47.5 203.0 %copy-start.61 = (f32[1536]{0:T(1024)}, f32[1536]{0:T(1024)S(1)}, u32[]{:S(2)}) copy-start(f32[1536]{0:T(1024)S(1)} %get-tuple-element.67) | copy-start | bytes 18436
  47.5 203.0 %copy-start.63 = (f32[1536]{0:T(1024)}, f32[1536]{0:T(1024)S(1)}, u32[]{:S(2)}) copy-start(f32[1536]{0:T(1024)S(1)} %get-tuple-element.68) | copy-start | bytes 18436
  47.5 203.0 %copy-start.65 = (f32[1536]{0:T(1024)}, f32[1536]{0:T(1024)S(1)}, u32[]{:S(2)}) copy-start(f32[1536]{0:T(1024)S(1)} %get-tuple-element.69) | copy-start | bytes 18436
  47.5 203.0 %copy-start.67 = (f32[1536]{0:T(1024)}, f32[1536]{0:T(1024)S(1)}, u32[]{:S(2)}) copy-start(f32[1536]{0:T(1024)S(1)} %get-tuple-element.70) | copy-start | bytes 18436
  47.5 203.0 %copy-start.69 = (f32[1536]{0:T(1024)}, f32[1536]{0:T(1024)S(1)}, u32[]{:S(2)}) copy-start(f32[1536]{0:T(1024)S(1)} %get-tuple-element.71) | copy-start | bytes 18436
  47.5 203.0 %copy-start.71 = (f32[1536]{0:T(1024)}, f32[1536]{0:T(1024)S(1)}, u32[]{:S(2)}) copy-start(f32[1536]{0:T(1024)S(1)} %get-tuple-element.72) | copy-start | bytes 18436
  47.5 203.0 %copy-start.73 = (f32[1536]{0:T(1024)}, f32[1536]{0:T(1024)S(1)}, u32[]{:S(2)}) copy-start(f32[1536]{0:T(1024)S(1)} %get-tuple-element.73) | copy-start | bytes 18436
  47.5 203.0 %copy-start.75 = (f32[1536]{0:T(1024)}, f32[1536]{0:T(1024)S(1)}, u32[]{:S(2)}) copy-start(f32[1536]{0:T(1024)S(1)} %get-tuple-element.74) | copy-start | bytes 18436
  47.5 203.0 %copy-start.77 = (f32[1536]{0:T(1024)}, f32[1536]{0:T(1024)S(1)}, u32[]{:S(2)}) copy-start(f32[1536]{0:T(1024)S(1)} %get-tuple-element.75) | copy-start | bytes 18436
  47.9 202.7 %copy-start.17 = (f32[1536]{0:T(1024)}, f32[1536]{0:T(1024)S(1)}, u32[]{:S(2)}) copy-start(f32[1536]{0:T(1024)S(1)} %get-tuple-element.45) | copy-start | bytes 18436
  47.9 202.7 %copy-start.19 = (f32[1536]{0:T(1024)}, f32[1536]{0:T(1024)S(1)}, u32[]{:S(2)}) copy-start(f32[1536]{0:T(1024)S(1)} %get-tuple-element.46) | copy-start | bytes 18436
  47.9 202.7 %copy-start.21 = (f32[1536]{0:T(1024)}, f32[1536]{0:T(1024)S(1)}, u32[]{:S(2)}) copy-start(f32[1536]{0:T(1024)S(1)} %get-tuple-element.47) | copy-start | bytes 18436
  47.9 202.7 %copy-start.23 = (f32[1536]{0:T(1024)}, f32[1536]{0:T(1024)S(1)}, u32[]{:S(2)}) copy-start(f32[1536]{0:T(1024)S(1)} %get-tuple-element.48) | copy-start | bytes 18436
  47.9 202.7 %copy-start.25 = (f32[1536]{0:T(1024)}, f32[1536]{0:T(1024)S(1)}, u32[]{:S(2)}) copy-start(f32[1536]{0:T(1024)S(1)} %get-tuple-element.49) | copy-start | bytes 18436
  47.9 202.7 %copy-start.27 = (f32[1536]{0:T(1024)}, f32[1536]{0:T(1024)S(1)}, u32[]{:S(2)}) copy-start(f32[1536]{0:T(1024)S(1)} %get-tuple-element.50) | copy-start | bytes 18436
  47.9 202.7 %copy-start.29 = (f32[1536]{0:T(1024)}, f32[1536]{0:T(1024)S(1)}, u32[]{:S(2)}) copy-start(f32[1536]{0:T(1024)S(1)} %get-tuple-element.51) | copy-start | bytes 18436
  47.9 202.7 %copy-start.31 = (f32[1536]{0:T(1024)}, f32[1536]{0:T(1024)S(1)}, u32[]{:S(2)}) copy-start(f32[1536]{0:T(1024)S(1)} %get-tuple-element.52) | copy-start | bytes 18436
  48.0 202.7 %copy-start.33 = (f32[1536]{0:T(1024)}, f32[1536]{0:T(1024)S(1)}, u32[]{:S(2)}) copy-start(f32[1536]{0:T(1024)S(1)} %get-tuple-element.53) | copy-start | bytes 18436
  48.0 202.7 %copy-start.35 = (f32[1536]{0:T(1024)}, f32[1536]{0:T(1024)S(1)}, u32[]{:S(2)}) copy-start(f32[1536]{0:T(1024)S(1)} %get-tuple-element.54) | copy-start | bytes 18436
  48.0 202.7 %copy-start.37 = (f32[1536]{0:T(1024)}, f32[1536]{0:T(1024)S(1)}, u32[]{:S(2)}) copy-start(f32[1536]{0:T(1024)S(1)} %get-tuple-element.55) | copy-start | bytes 18436
  48.0 202.7 %copy-start.39 = (f32[1536]{0:T(1024)}, f32[1536]{0:T(1024)S(1)}, u32[]{:S(2)}) copy-start(f32[1536]{0:T(1024)S(1)} %get-tuple-element.56) | copy-start | bytes 18436
  48.0 202.7 %copy-start.41 = (f32[1536]{0:T(1024)}, f32[1536]{0:T(1024)S(1)}, u32[]{:S(2)}) copy-start(f32[1536]{0:T(1024)S(1)} %get-tuple-element.57) | copy-start | bytes 18436
  48.0 202.7 %copy-start.43 = (f32[1536]{0:T(1024)}, f32[1536]{0:T(1024)S(1)}, u32[]{:S(2)}) copy-start(f32[1536]{0:T(1024)S(1)} %get-tuple-element.58) | copy-start | bytes 18436
  48.0 202.7 %copy-start.45 = (f32[1536]{0:T(1024)}, f32[1536]{0:T(1024)S(1)}, u32[]{:S(2)}) copy-start(f32[1536]{0:T(1024)S(1)} %get-tuple-element.59) | copy-start | bytes 18436
  48.0 202.7 %copy-start.47 = (f32[1536]{0:T(1024)}, f32[1536]{0:T(1024)S(1)}, u32[]{:S(2)}) copy-start(f32[1536]{0:T(1024)S(1)} %get-tuple-element.60) | copy-start | bytes 18436
  48.0 202.7 %copy-start.49 = (f32[1536]{0:T(1024)}, f32[1536]{0:T(1024)S(1)}, u32[]{:S(2)}) copy-start(f32[1536]{0:T(1024)S(1)} %get-tuple-element.61) | copy-start | bytes 18436
  48.0 202.7 %copy-start.51 = (f32[1536]{0:T(1024)}, f32[1536]{0:T(1024)S(1)}, u32[]{:S(2)}) copy-start(f32[1536]{0:T(1024)S(1)} %get-tuple-element.62) | copy-start | bytes 18436
  48.0 202.7 %copy-start.53 = (f32[1536]{0:T(1024)}, f32[1536]{0:T(1024)S(1)}, u32[]{:S(2)}) copy-start(f32[1536]{0:T(1024)S(1)} %get-tuple-element.63) | copy-start | bytes 18436
  52.8 197.9 %copy-start.85 = (f32[384]{0:T(512)}, f32[384]{0:T(512)S(1)}, u32[]{:S(2)}) copy-start(f32[384]{0:T(512)S(1)} %get-tuple-element.91) | copy-start | bytes 4612
  52.8 197.9 %copy-start.88 = (f32[384]{0:T(512)}, f32[384]{0:T(512)S(1)}, u32[]{:S(2)}) copy-start(f32[384]{0:T(512)S(1)} %get-tuple-element.92) | copy-start | bytes 4612
  52.9 197.9 %copy-start.92 = (f32[384]{0:T(512)}, f32[384]{0:T(512)S(1)}, u32[]{:S(2)}) copy-start(f32[384]{0:T(512)S(1)} %get-tuple-element.93) | copy-start | bytes 4612
  56.5 219.3 %copy-start.2 = (bf16[384,1536]{1,0:T(8,128)(2,1)}, bf16[384,1536]{1,0:T(8,128)(2,1)S(1)}, u32[]{:S(2)}) copy-start(bf16[384,1536]{1,0:T(8,128)(2,1)S(1)} %scatter_custom_fusion) | copy-start | bytes 3538948
  242.6 5.4 collective-permute-start
  245.6 4.8 collective-permute-start.3
  288.0 5.8 collective-permute-start.4
  292.1 5.7 collective-permute-start.5
  333.5 566.0 %all-reduce.6.cloned.1.call-start = ((), (), s32[]{:S(2)}) async-start(), calls=%async_computation.5 | async-start | bytes 393216 | tf_op jit(solution)/shard_map/psum | solution.py:128
  372.9 332.6 %copy-start.4 = (bf16[384,1536]{1,0:T(8,128)(2,1)S(1)}, bf16[384,1536]{1,0:T(8,128)(2,1)}, u32[]{:S(2)}) copy-start(bf16[384,1536]{1,0:T(8,128)(2,1)} %copy-done.2) | copy-start | bytes 3538948
  372.9 332.6 %copy-start.6 = (bf16[384,1536]{1,0:T(8,128)(2,1)S(1)}, bf16[384,1536]{1,0:T(8,128)(2,1)}, u32[]{:S(2)}) copy-start(bf16[384,1536]{1,0:T(8,128)(2,1)} %get-tuple-element.110) | copy-start | bytes 3538948
  379.0 815.0 %all-reduce.4.cloned.1.call-start = ((), (), s32[]{:S(2)}) async-start(), calls=%async_computation.4 | async-start | bytes 4718592 | tf_op jit(solution)/shard_map/psum | solution.py:120
  (60 other events, 1639.0 us)
Sparse Core Ops, SparseCore 0:
  29.9 2.7 sort.30.cloned.1.call-done
  379.1 520.3 all-reduce.5
  902.3 291.6 all-reduce.3
  (1 shorter events, 0.0 us)
Sparse Core Ops, SparseCore 1:
  32.0 203.2 all-gather.2
  333.6 371.8 reduce-scatter.1
where the time goes:
time: 1210 us
  waiting for transfers between devices  909 us (75%)
  blocking collectives  99.1 us (8%)
  other arithmetic  96.2 us (8%)
  local copies, waits for them, and re-layouts  37 us (3%)
  matrix products  26.4 us (2%)
  starting transfers between devices  20.1 us (2%)
  between operations  17.2 us (1%)
    reduce_scatter x1, waiting for transfers between devices, on_device(): lax.psum_scatter(jnp.dot(normed.T, d_proj, preferred_element_type=jnp.flo...  326 us
    psum x1, waiting for transfers between devices, on_device(): grad_weight = lax.psum(replica_shard, 'dp')  295 us
    all_gather x1, waiting for transfers between devices, on_device(): lax.all_gather(w_glu, 'fsdp', axis=0, tiled=True)  178 us
    psum x1, waiting for transfers between devices, on_device(): lax.psum((g_gain_in, g_kernel, g_gain_mid), ('dp', 'fsdp'))  99.8 us
    psum x1, blocking collectives, on_device(): lax.psum((g_gain_in, g_kernel, g_gain_mid), ('dp', 'fsdp'))  78.8 us
    reduce_sum x6, other arithmetic, kernel_grad(): jnp.sum(upstream * extended[j:j + width].astype(jnp.float32) * masks[:, j...  31.1 us
    another operation x2, other arithmetic  24.8 us
    reduce_sum x2, other arithmetic, norm_rows(): centre = values - jnp.mean(values, axis=-1, keepdims=True)  24.8 us
  transfers between devices with their start and end apart: 11, of which 8 were waited for; matrix products, arithmetic and copies ran while one was open for 6% of the time, Pallas kernels for 0%

commit v1 on v0

v1 whole, which is shorter than its diff:
```python
import jax
import jax.numpy as jnp
from jax import lax
from jax.experimental import pallas as pl
from jax.experimental.pallas import tpu as pltpu
from jax.sharding import PartitionSpec as P

EPS = 1e-05
ROWS = 384
D = 1536
TAPS = 31
MESH = pl.DeviceIdType.MESH
F32 = jnp.float32
BF16 = jnp.bfloat16
VMEM_LIMIT = 56 * 1024 * 1024


def place():
    dp = lax.axis_index("dp")
    me = lax.axis_index("fsdp")
    z_hi = lax.div(dp, 8)
    x = lax.rem(lax.div(dp, 2), 4)
    core = lax.rem(dp, 2)
    return dp, me, z_hi, x, core, lax.div(me, 2), lax.rem(me, 2)


def send(src, dst, send_sem, recv_sem, target):
    copy = pltpu.make_async_remote_copy(
        src_ref=src, dst_ref=dst, send_sem=send_sem, recv_sem=recv_sem, device_id=target, device_id_type=MESH
    )
    copy.start()
    return copy


def greet(targets):
    barrier = pltpu.get_barrier_semaphore()
    for target in targets:
        pl.semaphore_signal(barrier, inc=1, device_id=target, device_id_type=MESH)
    pl.semaphore_wait(barrier, len(targets))


def vec_mean(v):
    return jnp.sum(v, axis=-1, keepdims=True) * (1.0 / D)


def front_kernel(
    frames, dest, seg, w, gain, cot,
    packed, normed_t, w_out, value, sig, gext, cext, sext,
    w_all, out_buf, in_buf, normed, a_s, a_r, y_s, y_r, z_s, z_r, b_s, b_r, h_s, h_r, l_s,
):
    dp, me, z_hi, x, core, y, z_lo = place()
    sib = (dp + 1 - 2 * core, me)
    up = (lax.rem(z_hi + z_lo, 4) * 8 + x * 2 + core, me + 1 - 2 * z_lo)
    down = (lax.rem(z_hi + 3 + z_lo, 4) * 8 + x * 2 + core, me + 1 - 2 * z_lo)
    far = (lax.rem(z_hi + 3 + 2 * z_lo, 4) * 8 + x * 2 + core, me + 1 - 2 * z_lo)
    nxt = (dp, lax.rem(me + 1, 8))
    prv = (dp, lax.rem(me + 7, 8))

    greet([(dp, lax.rem(me + s, 8)) for s in range(1, 8)] + [far, sib])

    half = core * 96
    y_copies = []
    for s in (1, 3, 2):
        peer = (dp, 2 * lax.rem(y + s, 4) + z_lo)
        y_copies.append(
            send(
                w.at[pl.ds(half, 96), :],
                w_all.at[pl.ds(192 * me + half, 96), :],
                y_s.at[s - 1], y_r.at[s - 1], peer,
            )
        )
    z_copies = [
        send(
            w.at[pl.ds(half + 48, 48), :], w_all.at[pl.ds(192 * me + half + 48, 48), :],
            z_s.at[0, 0], z_r.at[0, 0], up,
        ),
        send(
            w.at[pl.ds(half, 48), :], w_all.at[pl.ds(192 * me + half, 48), :],
            z_s.at[1, 0], z_r.at[1, 0], down,
        ),
    ]
    sext[32:416, :] = seg[...]
    halos = [
        send(cot.at[368:384, :], cext.at[0:16, :], h_s.at[0], h_r.at[0], nxt),
        send(cot.at[0:16, :], cext.at[400:416, :], h_s.at[1], h_r.at[1], prv),
        send(sext.at[384:416, :], sext.at[0:32, :], h_s.at[2], h_r.at[2], nxt),
        send(sext.at[32:64, :], sext.at[416:448, :], h_s.at[3], h_r.at[3], prv),
    ]
    cot_copy = pltpu.make_async_copy(cot, cext.at[16:400, :], l_s.at[0])
    cot_copy.start()

    d = dest[...]
    k8 = lax.broadcasted_iota(jnp.int32, (8, ROWS), 0)
    rel = d - ROWS * k8
    hot = jnp.logical_and(rel >= 0, rel < ROWS)
    hot_f = jnp.where(hot, 1.0, 0.0).astype(F32)
    before = lax.broadcasted_iota(jnp.int32, (ROWS, ROWS), 0) < lax.broadcasted_iota(jnp.int32, (ROWS, ROWS), 1)
    rank = jnp.dot(hot_f.astype(BF16), jnp.where(before, 1.0, 0.0).astype(BF16), preferred_element_type=F32)
    order = jnp.sum(hot_f * (rank + 48.0 * k8.astype(F32)), axis=0, keepdims=True)
    slot = jnp.sum(hot_f * rel.astype(F32), axis=0, keepdims=True)
    high = jnp.floor(slot * (1.0 / 16.0))
    low = slot - 16.0 * high
    row_id = lax.broadcasted_iota(jnp.int32, (ROWS, ROWS), 0).astype(F32)
    perm = jnp.where(row_id == order, 1.0, 0.0).astype(BF16)
    tag_row = lax.broadcasted_iota(jnp.int32, (128, ROWS), 0)
    tags = jnp.where(tag_row == 0, high, jnp.where(tag_row == 1, low, 0.0)).astype(BF16)
    out_buf[:, D:] = lax.dot_general(perm, tags, (((1,), (1,)), ((), ())), preferred_element_type=F32).astype(BF16)
    for c in range(3):
        out_buf[:, 512 * c : 512 * c + 512] = jnp.dot(
            perm, frames[:, 512 * c : 512 * c + 512], preferred_element_type=F32
        ).astype(BF16)
    a_copies = []
    for s in (1, 7, 2, 6, 3, 5, 4):
        peer = lax.rem(me + s, 8)
        a_copies.append(
            send(
                out_buf.at[pl.ds(48 * peer, 48), :], in_buf.at[pl.ds(48 * me, 48), :],
                a_s.at[s - 1], a_r.at[s - 1], (dp, peer),
            )
        )
    own = pltpu.make_async_copy(out_buf.at[pl.ds(48 * me, 48), :], in_buf.at[pl.ds(48 * me, 48), :], l_s.at[1])
    own.start()
    own_w = pltpu.make_async_copy(w, w_all.at[pl.ds(192 * me, 192), :], l_s.at[2])
    own_w.start()

    b_copies = []

    def pass_on(shard, index):
        piece = w_all.at[pl.ds(192 * shard + half, 96), :]
        b_copies.append(send(piece, piece, b_s.at[index], b_r.at[index], sib))

    def y_arrived(n, s):
        y_copies[n].wait_recv()
        shard = 2 * lax.rem(y + 4 - s, 4) + z_lo
        base = 192 * shard + half
        top = w_all.at[pl.ds(base + 48, 48), :]
        low_rows = w_all.at[pl.ds(base, 48), :]
        z_copies.append(send(top, top, z_s.at[0, s], z_r.at[0, s], up))
        z_copies.append(send(low_rows, low_rows, z_s.at[1, s], z_r.at[1, s], down))
        pass_on(shard, s - 1)

    y_arrived(0, 1)
    y_arrived(1, 3)

    own.wait()
    for copy in a_copies:
        copy.wait_recv()
    tag = in_buf[:, D:].astype(F32)
    at = tag[:, 0:1] * 16.0 + tag[:, 1:2]
    col_id = lax.broadcasted_iota(jnp.int32, (ROWS, ROWS), 1).astype(F32)
    unperm = jnp.where(col_id == at, 1.0, 0.0).T.astype(BF16)
    for c in range(3):
        packed[:, 512 * c : 512 * c + 512] = jnp.dot(
            unperm, in_buf[:, 512 * c : 512 * c + 512], preferred_element_type=F32
        ).astype(BF16)

    def norm_body(i, carry):
        rows = pl.ds(pl.multiple_of(32 * i, 32), 32)
        v = packed[rows, :].astype(F32)
        centre = v - vec_mean(v)
        scale = lax.rsqrt(vec_mean(centre * centre) + EPS)
        normed[rows, :] = (centre * scale * gain[...]).astype(BF16)
        return carry

    lax.fori_loop(0, 12, norm_body, 0)
    for c in range(4):
        flipped = normed[:, 384 * c : 384 * c + 384].astype(F32).T.astype(BF16)
        for z in range(2):
            for p in range(2):
                to = 768 * p + 192 * c + 96 * z
                normed_t[to : to + 96, :] = flipped[192 * z + 96 * p : 192 * z + 96 * p + 96, :]

    y_arrived(2, 2)
    for n, t in enumerate((0, 1, 3, 2)):
        z_copies[2 * n].wait_recv()
        z_copies[2 * n + 1].wait_recv()
        pass_on(2 * lax.rem(y + 4 - t, 4) + 1 - z_lo, 3 + t)
    own_w.wait()
    for copy in b_copies:
        copy.wait_recv()
    w_copy = pltpu.make_async_copy(w_all, w_out, l_s.at[3])
    w_copy.start()

    def proj_body(i, carry):
        left = pl.ds(pl.multiple_of(256 * i, 256), 256)
        right = pl.ds(pl.multiple_of(256 * i + D, 256), 256)
        v = jnp.dot(normed[...], w_all[:, left], preferred_element_type=F32)
        g = jnp.dot(normed[...], w_all[:, right], preferred_element_type=F32)
        s = jax.nn.sigmoid(g)
        value[:, left] = v
        sig[:, left] = s
        gext[32:416, left] = (v * s).astype(BF16)
        return carry

    lax.fori_loop(0, 6, proj_body, 0)
    halos.append(send(gext.at[384:416, :], gext.at[0:32, :], h_s.at[4], h_r.at[4], nxt))
    halos.append(send(gext.at[32:64, :], gext.at[416:448, :], h_s.at[5], h_r.at[5], prv))
    cot_copy.wait()
    w_copy.wait()
    for copy in halos:
        copy.wait()
    for copy in a_copies + y_copies + z_copies + b_copies:
        copy.wait_send()


def front(frames, dest, seg, w, gain, cot):
    vm = pl.BlockSpec(memory_space=pltpu.VMEM)
    hbm = pl.BlockSpec(memory_space=pl.ANY)
    sems = pltpu.SemaphoreType.DMA
    return pl.pallas_call(
        front_kernel,
        out_shape=(
            jax.ShapeDtypeStruct((ROWS, D), BF16),
            jax.ShapeDtypeStruct((D, ROWS), BF16),
            jax.ShapeDtypeStruct((D, 2 * D), BF16),
            jax.ShapeDtypeStruct((ROWS, D), F32),
            jax.ShapeDtypeStruct((ROWS, D), F32),
            jax.ShapeDtypeStruct((448, D), BF16),
            jax.ShapeDtypeStruct((416, D), BF16),
            jax.ShapeDtypeStruct((448, 128), jnp.int32),
        ),
        in_specs=[vm] * 6,
        out_specs=(vm, vm, hbm, vm, vm, vm, vm, vm),
        scratch_shapes=[
            pltpu.VMEM((D, 2 * D), BF16),
            pltpu.VMEM((ROWS, D + 128), BF16),
            pltpu.VMEM((ROWS, D + 128), BF16),
            pltpu.VMEM((ROWS, D), BF16),
            sems((7,)), sems((7,)),
            sems((3,)), sems((3,)),
            sems((2, 4)), sems((2, 4)),
            sems((7,)), sems((7,)),
            sems((6,)), sems((6,)),
            sems((4,)),
        ],
        compiler_params=pltpu.CompilerParams(
            collective_id=0, has_side_effects=True, vmem_limit_bytes=VMEM_LIMIT
        ),
        name="front",
    )(frames, dest, seg, w, gain, cot)


def middle_kernel(
    gext, packed, cext, sext, kern, gain, value, sig,
    output, d_proj, small,
    gx, mx, kb, gk, seg,
):
    me = lax.axis_index("fsdp")
    edge = lax.broadcasted_iota(jnp.int32, (448, 128), 0) + ROWS * me - 32
    seg[...] = jnp.where(jnp.logical_and(edge >= 0, edge < 8 * ROWS), sext[...], -1)
    for l in range(12):
        gx[l] = gext[:, 128 * l : 128 * l + 128].astype(F32)
        for j in range(TAPS):
            kb[l, j] = jnp.broadcast_to(kern[j : j + 1, 128 * l : 128 * l + 128], (8, 128))
    gk[...] = jnp.zeros_like(gk)

    def uneven(first, last):
        return jnp.max(jnp.abs(seg[pl.ds(first, 1), :] - seg[pl.ds(last, 1), :])) > 0

    def conv(base, l, masked):
        total = [jnp.zeros((8, 128), F32) for _ in range(4)]
        if masked:
            here = [seg[pl.ds(base + 16 + 8 * t, 8), :] for t in range(4)]
        for j in range(TAPS):
            k = kb[l, j]
            for t in range(4):
                at = pl.ds(base + 1 + j + 8 * t, 8)
                v = gx[l, at, :]
                if masked:
                    v = jnp.where(seg[at, :] == here[t], v, 0.0)
                total[t] = total[t] + v * k
        for t in range(4):
            mx[l, pl.ds(base + 8 * t, 8), :] = total[t]

    def conv_block(b, carry):
        base = pl.multiple_of(32 * b, 32)
        mixed_up = uneven(base + 1, base + 62)

        @pl.when(mixed_up)
        def _():
            lax.fori_loop(0, 12, lambda l, c: (conv(base, l, True), c)[1], 0)

        @pl.when(jnp.logical_not(mixed_up))
        def _():
            lax.fori_loop(0, 12, lambda l, c: (conv(base, l, False), c)[1], 0)

        return carry

    lax.fori_loop(0, 13, conv_block, 0)

    def row_mean(parts):
        total = parts[0]
        for part in parts[1:]:
            total = total + part
        return jnp.sum(total, axis=-1, keepdims=True) * (1.0 / D)

    def norm_block(i, acc):
        base = pl.multiple_of(16 * i, 16)
        rows = pl.ds(base, 16)
        mixed = [mx[l, rows, :] for l in range(12)]
        mean = row_mean(mixed)
        centre = [m - mean for m in mixed]
        scale = lax.rsqrt(row_mean([c * c for c in centre]) + EPS)
        own = jnp.logical_and(i > 0, i < 25)
        acc_new = []
        e_all, unit_all = [], []
        back = pl.ds(pl.multiple_of(jnp.clip(base - 16, 0, ROWS - 16), 16), 16)
        for l in range(12):
            cols = slice(128 * l, 128 * l + 128)
            unit = centre[l] * scale
            mid = unit * gain[0:1, cols]
            s = jax.nn.sigmoid(mid)
            gated = mid * s

            @pl.when(own)
            def _():
                output[back, cols] = (packed[back, cols].astype(F32) + gated).astype(BF16)

            d_mid = cext[rows, cols].astype(F32) * (s + gated * (1.0 - s))
            du = d_mid * unit
            acc_new.append(acc[l] + jnp.where(own, du[0:8] + du[8:16], 0.0))
            e_all.append(d_mid * gain[0:1, cols])
            unit_all.append(unit)
        e_mean = row_mean(e_all)
        eu_mean = row_mean([e * u for e, u in zip(e_all, unit_all)])
        for l in range(12):
            mx[l, rows, :] = scale * (e_all[l] - e_mean - unit_all[l] * eu_mean)
        return tuple(acc_new)

    gain_acc = lax.fori_loop(0, 26, norm_block, tuple(jnp.zeros((8, 128), F32) for _ in range(12)))

    def conv_back(base, l, masked):
        total = [jnp.zeros((8, 128), F32) for _ in range(4)]
        glu = [gx[l, pl.ds(base + 32 + 8 * t, 8), :] for t in range(4)]
        if masked:
            here = [seg[pl.ds(base + 32 + 8 * t, 8), :] for t in range(4)]
        for j in range(TAPS):
            k = kb[l, TAPS - 1 - j]
            tap = None
            for t in range(4):
                v = mx[l, pl.ds(base + 1 + j + 8 * t, 8), :]
                if masked:
                    v = jnp.where(seg[pl.ds(base + 17 + j + 8 * t, 8), :] == here[t], v, 0.0)
                total[t] = total[t] + v * k
                tap = glu[t] * v if tap is None else tap + glu[t] * v
            gk[l, TAPS - 1 - j] += tap
        cols = pl.ds(pl.multiple_of(128 * l, 128), 128)
        for t in range(2):
            rows = pl.ds(base + 16 * t, 16)
            d_glu = jnp.concatenate([total[2 * t], total[2 * t + 1]], axis=0)
            s = sig[rows, cols]
            d_value = d_glu * s
            d_proj[0, rows, cols] = d_value.astype(BF16)
            d_proj[1, rows, cols] = (d_value * value[rows, cols] * (1.0 - s)).astype(BF16)

    def back_block(b, carry):
        base = pl.multiple_of(32 * b, 32)
        mixed_up = uneven(base + 17, base + 78)

        @pl.when(mixed_up)
        def _():
            lax.fori_loop(0, 12, lambda l, c: (conv_back(base, l, True), c)[1], 0)

        @pl.when(jnp.logical_not(mixed_up))
        def _():
            lax.fori_loop(0, 12, lambda l, c: (conv_back(base, l, False), c)[1], 0)

        return carry

    lax.fori_loop(0, 12, back_block, 0)
    for l in range(12):
        cols = slice(128 * l, 128 * l + 128)
        for j in range(TAPS):
            small[j : j + 1, cols] = jnp.sum(gk[l, j], axis=0, keepdims=True)
        small[TAPS : TAPS + 1, cols] = jnp.sum(gain_acc[l], axis=0, keepdims=True)


def middle(gext, packed, cext, sext, kern, gain, value, sig):
    vm = pl.BlockSpec(memory_space=pltpu.VMEM)
    return pl.pallas_call(
        middle_kernel,
        out_shape=(
            jax.ShapeDtypeStruct((ROWS, D), BF16),
            jax.ShapeDtypeStruct((2, ROWS, D), BF16),
            jax.ShapeDtypeStruct((32, D), F32),
        ),
        in_specs=[vm] * 8,
        out_specs=(vm, vm, vm),
        scratch_shapes=[
            pltpu.VMEM((12, 448, 128), F32),
            pltpu.VMEM((12, 416, 128), F32),
            pltpu.VMEM((12, TAPS, 8, 128), F32),
            pltpu.VMEM((12, TAPS, 8, 128), F32),
            pltpu.VMEM((448, 128), jnp.int32),
        ],
        compiler_params=pltpu.CompilerParams(vmem_limit_bytes=VMEM_LIMIT),
        name="middle",
    )(gext, packed, cext, sext, kern, gain, value, sig)


def back_kernel(
    normed_t, d_proj, w, packed, gain, cot, small_in,
    grad_frames, w_grad, small,
    ncat, pcat, dn, p0, p1, r0, r1, e0, e1, s0, s1, f, t_in, g, u_in, sa, sb, sy, sx, sz,
    c_s, c_r, q0_s, q0_r, q1_s, q1_r, m0_s, m0_r, m1_s, m1_r, z_s, z_r, u_s, u_r, v_s, v_r, x_s, x_r,
    k_s, k_r, ky_s, ky_r, kx_s, kx_r, kz_s, kz_r,
):
    dp, me, z_hi, x, core, y, z_lo = place()
    sib = (dp + 1 - 2 * core, me)
    pair = (dp, me + 1 - 2 * z_lo)

    def x_of(s):
        return lax.rem(x + s, 4)

    def y_of(s):
        return lax.rem(y + s, 4)

    def z_of(s):
        return lax.rem(z_hi + s, 4)

    def x_dev(s):
        return (z_hi * 8 + x_of(s) * 2 + core, me)

    def y_dev(s):
        return (dp, 2 * y_of(s) + z_lo)

    def z_dev(s):
        return (z_of(s) * 8 + x * 2 + core, me)

    steps = (1, 3, 2)
    greet(
        [sib, pair] + [x_dev(s) for s in steps] + [y_dev(s) for s in steps] + [z_dev(s) for s in steps]
    )
    sends = []

    core_copies = [
        send(normed_t, ncat.at[:, 384:768], c_s.at[0], c_r.at[0], sib),
        send(d_proj.at[1 - core], pcat.at[384:768, :], c_s.at[1], c_r.at[1], sib),
    ]
    sends += core_copies
    ncat[:, 0:384] = normed_t[...]
    pcat[0:384, :] = d_proj[core]

    def dn_body(i, carry):
        cols = pl.ds(pl.multiple_of(256 * i, 256), 256)
        dims = (((1,), (1,)), ((), ()))
        dn[:, cols] = lax.dot_general(
            d_proj[0], w[cols, 0:D], dims, preferred_element_type=F32
        ) + lax.dot_general(d_proj[1], w[cols, D : 2 * D], dims, preferred_element_type=F32)
        return carry

    lax.fori_loop(0, 6, dn_body, 0)
    for copy in core_copies:
        copy.wait_recv()

    stage0, stage1 = [], []
    for s in (1, 3, 2, 0):
        rows = pl.ds(pl.multiple_of(192 * y_of(s), 64), 192)

        def body0(i, carry, rows=rows):
            cols = pl.ds(pl.multiple_of(512 * i, 512), 512)
            p0[rows, cols] = jnp.dot(ncat[rows, :], pcat[:, cols], preferred_element_type=F32).astype(BF16)
            return carry

        lax.fori_loop(0, 3, body0, 0)
        if s:
            stage0.append(send(p0.at[rows, :], r0.at[s - 1], q0_s.at[s - 1], q0_r.at[s - 1], y_dev(s)))
        where = x_of(s)
        cols1 = pl.ds(pl.multiple_of(384 * where, 128), 384)

        def body1(i, carry, cols1=cols1, where=where):
            rows1 = pl.multiple_of(256 * i, 256)
            p1[where, pl.ds(rows1, 256), :] = jnp.dot(
                ncat[pl.ds(768 + rows1, 256), :], pcat[:, cols1], preferred_element_type=F32
            ).astype(BF16)
            return carry

        lax.fori_loop(0, 3, body1, 0)
        if s:
            stage1.append(send(p1.at[where], r1.at[s - 1], q1_s.at[s - 1], q1_r.at[s - 1], x_dev(s)))

    def frames_body(i, acc):
        rows = pl.ds(pl.multiple_of(16 * i, 16), 16)
        v = packed[rows, :].astype(F32)
        centre = v - vec_mean(v)
        scale = lax.rsqrt(vec_mean(centre * centre) + EPS)
        unit = centre * scale
        up = dn[rows, :]
        du = up * unit
        e = up * gain[...]
        back = scale * (e - vec_mean(e) - unit * vec_mean(e * unit))
        grad_frames[rows, :] = (cot[rows, :].astype(F32) + back).astype(BF16)
        return acc + du[0:8, :] + du[8:16, :]

    gain_acc = lax.fori_loop(0, 24, frames_body, jnp.zeros((8, D), F32))

    sa[0:32, :] = small_in[...]
    sa[32:40, :] = jnp.where(
        lax.broadcasted_iota(jnp.int32, (8, D), 0) == 0, jnp.sum(gain_acc, axis=0, keepdims=True), 0.0
    )
    mine = pl.multiple_of(768 * core, 128)
    other = pl.multiple_of(768 - 768 * core, 128)
    copy = send(sa.at[:, pl.ds(other, 768)], sb.at[:, 0:768], k_s.at[0], k_r.at[0], sib)
    sends.append(copy)
    copy.wait_recv()
    sb[:, 768:1536] = sb[:, 0:768] + sa[:, pl.ds(mine, 768)]
    z_mine = pl.multiple_of(768 + 384 * z_lo, 128)
    z_other = pl.multiple_of(768 + 384 - 384 * z_lo, 128)
    copy = send(sb.at[:, pl.ds(z_other, 384)], sy.at[4], k_s.at[1], k_r.at[1], pair)
    sends.append(copy)
    copy.wait_recv()
    sy[pl.ds(y, 1)] = (sb[:, pl.ds(z_mine, 384)] + sy[4])[None]
    y_small = [send(sy.at[y], sy.at[y], ky_s.at[s - 1], ky_r.at[s - 1], y_dev(s)) for s in steps]
    sends += y_small

    for copy in stage0:
        copy.wait_recv()
    rows = pl.ds(pl.multiple_of(192 * y, 64), 192)
    for c in range(3):
        cols = slice(512 * c, 512 * c + 512)
        e0[:, cols] = (
            p0[rows, cols].astype(F32) + r0[0, :, cols].astype(F32) + r0[1, :, cols].astype(F32) + r0[2, :, cols].astype(F32)
        ).astype(BF16)
    second0 = [
        send(
            e0.at[:, pl.ds(pl.multiple_of(384 * x_of(s), 128), 384)], s0.at[s - 1],
            m0_s.at[s - 1], m0_r.at[s - 1], x_dev(s),
        )
        for s in steps
    ]
    for copy in stage1:
        copy.wait_recv()
    for c in range(3):
        rows_c = slice(256 * c, 256 * c + 256)
        e1[rows_c, :] = (
            p1[x, rows_c, :].astype(F32) + r1[0, rows_c, :].astype(F32) + r1[1, rows_c, :].astype(F32) + r1[2, rows_c, :].astype(F32)
        ).astype(BF16)
    second1 = [
        send(
            e1.at[pl.ds(pl.multiple_of(192 * y_of(s), 64), 192), :], s1.at[s - 1],
            m1_s.at[s - 1], m1_r.at[s - 1], y_dev(s),
        )
        for s in steps
    ]
    for copy in y_small:
        copy.wait_recv()
    sx[pl.ds(x, 1)] = (sy[0] + sy[1] + sy[2] + sy[3])[None]
    x_small = [send(sx.at[x], sx.at[x], kx_s.at[s - 1], kx_r.at[s - 1], x_dev(s)) for s in steps]
    sends += stage0 + stage1 + second0 + second1 + x_small

    for copy in second0:
        copy.wait_recv()
    own0 = e0[:, pl.ds(pl.multiple_of(384 * x, 128), 384)].astype(F32)
    sum0 = (own0 + s0[0].astype(F32) + s0[1].astype(F32) + s0[2].astype(F32)).astype(BF16)
    f[0, 0:96, :] = sum0[0:96, :]
    f[1, 0:96, :] = sum0[96:192, :]
    for copy in second1:
        copy.wait_recv()
    own1 = e1[rows, :].astype(F32)
    sum1 = (own1 + s1[0].astype(F32) + s1[1].astype(F32) + s1[2].astype(F32)).astype(BF16)
    f[0, 96:192, :] = sum1[0:96, :]
    f[1, 96:192, :] = sum1[96:192, :]
    third = send(f.at[1 - z_lo], t_in, z_s.at[0], z_r.at[0], pair)
    sends.append(third)
    for copy in x_small:
        copy.wait_recv()
    sz[pl.ds(z_hi, 1)] = (sx[0] + sx[1] + sx[2] + sx[3])[None]
    z_small = [send(sz.at[z_hi], sz.at[z_hi], kz_s.at[s - 1], kz_r.at[s - 1], z_dev(s)) for s in steps]
    sends += z_small
    third.wait_recv()
    g[...] = (f[z_lo].astype(F32) + t_in[...].astype(F32)).astype(BF16)

    fourth = [
        send(
            g.at[pl.ds(pl.multiple_of(48 * z_of(s), 16), 48), :], u_in.at[s - 1],
            u_s.at[s - 1], u_r.at[s - 1], z_dev(s),
        )
        for s in steps
    ]
    sends += fourth
    for copy in z_small:
        copy.wait_recv()
    sb[:, 0:384] = sz[0] + sz[1] + sz[2] + sz[3]
    col_here = pl.multiple_of(768 * core + 384 * z_lo, 128)
    small[:, pl.ds(col_here, 384)] = sb[:, 0:384]
    here = small.at[:, pl.ds(col_here, 384)]
    small_z = send(here, here, k_s.at[2], k_r.at[2], pair)
    sends.append(small_z)
    for copy in fourth:
        copy.wait_recv()
    z_rows = pl.ds(pl.multiple_of(48 * z_hi, 16), 48)
    x_cols = pl.ds(pl.multiple_of(384 * x, 128), 384)
    w_grad[pl.ds(core, 1), z_rows, x_cols] = (
        g[z_rows, :].astype(F32) + u_in[0].astype(F32) + u_in[1].astype(F32) + u_in[2].astype(F32)
    ).astype(BF16)[None]
    piece = w_grad.at[core, z_rows, x_cols]
    fifth = [send(piece, piece, v_s.at[s - 1], v_r.at[s - 1], z_dev(s)) for s in steps]
    sends += fifth
    small_z.wait_recv()
    half = small.at[:, pl.ds(mine, 768)]
    small_c = send(half, half, k_s.at[3], k_r.at[3], sib)
    sends.append(small_c)
    for copy in fifth:
        copy.wait_recv()

    piece = w_grad.at[core, :, x_cols]
    sixth = [send(piece, piece, x_s.at[s - 1], x_r.at[s - 1], x_dev(s)) for s in steps]
    sends += sixth
    for copy in sixth:
        copy.wait_recv()
    last = send(w_grad.at[core], w_grad.at[core], c_s.at[2], c_r.at[2], sib)
    sends.append(last)
    small_c.wait_recv()
    last.wait_recv()
    for copy in sends:
        copy.wait_send()


def back(normed_t, d_proj, w, packed, gain, cot, small_in):
    vm = pl.BlockSpec(memory_space=pltpu.VMEM)
    sems = pltpu.SemaphoreType.DMA
    three = [sems((3,)), sems((3,))]
    return pl.pallas_call(
        back_kernel,
        out_shape=(
            jax.ShapeDtypeStruct((ROWS, D), BF16),
            jax.ShapeDtypeStruct((2, 192, D), BF16),
            jax.ShapeDtypeStruct((40, D), F32),
        ),
        in_specs=[vm] * 7,
        out_specs=(vm, vm, vm),
        scratch_shapes=[
            pltpu.VMEM((D, 768), BF16),
            pltpu.VMEM((768, D), BF16),
            pltpu.VMEM((ROWS, D), F32),
            pltpu.VMEM((768, D), BF16),
            pltpu.VMEM((4, 768, 384), BF16),
            pltpu.VMEM((3, 192, D), BF16),
            pltpu.VMEM((3, 768, 384), BF16),
            pltpu.VMEM((192, D), BF16),
            pltpu.VMEM((768, 384), BF16),
            pltpu.VMEM((3, 192, 384), BF16),
            pltpu.VMEM((3, 192, 384), BF16),
            pltpu.VMEM((2, 192, 384), BF16),
            pltpu.VMEM((192, 384), BF16),
            pltpu.VMEM((192, 384), BF16),
            pltpu.VMEM((3, 48, 384), BF16),
            pltpu.VMEM((40, D), F32),
            pltpu.VMEM((40, D), F32),
            pltpu.VMEM((5, 40, 384), F32),
            pltpu.VMEM((4, 40, 384), F32),
            pltpu.VMEM((4, 40, 384), F32),
            sems((3,)), sems((3,)),
            *three, *three, *three, *three,
            sems((1,)), sems((1,)),
            *three, *three, *three,
            sems((4,)), sems((4,)),
            *three, *three, *three,
        ],
        compiler_params=pltpu.CompilerParams(
            collective_id=1, has_side_effects=True, vmem_limit_bytes=VMEM_LIMIT
        ),
        name="back",
    )(normed_t, d_proj, w, packed, gain, cot, small_in)


def on_device(frames_in, dest, segment, gain_in, w_glu, kernel, gain_mid, cotangent):
    seg = jnp.broadcast_to(segment.reshape(ROWS, 1), (ROWS, 128))
    gain = gain_in.reshape(1, D)
    packed, normed_t, w, value, sig, gext, cext, sext = front(
        frames_in, dest.reshape(1, ROWS), seg, w_glu, gain, cotangent
    )
    output, d_proj, small_in = middle(
        gext, packed, cext, sext, kernel, gain_mid.reshape(1, D), value, sig
    )
    grad_frames, w_grad, small = back(normed_t, d_proj, w, packed, gain, cotangent, small_in)
    grad_weight = jnp.concatenate([w_grad[0], w_grad[1]], axis=1).astype(F32)
    return (output, grad_frames, grad_weight, small[32], small[:TAPS], small[TAPS])


def solution(mesh):
    return jax.shard_map(
        on_device,
        mesh=mesh,
        in_specs=(
            P(("dp", "fsdp"), None),
            P(("dp", "fsdp")),
            P("dp", "fsdp"),
            P(),
            P("fsdp", None),
            P(),
            P(),
            P(("dp", "fsdp"), None),
        ),
        out_specs=(
            P(("dp", "fsdp"), None),
            P(("dp", "fsdp"), None),
            P("fsdp", None),
            P(),
            P(),
            P(),
        ),
        check_vma=False,
    )
```

time: 1210 us -> 227 us (0.19)
  waiting for transfers between devices: 909 us -> 0 us
  Pallas kernels: 0 us -> 214 us
  blocking collectives: 99.1 us -> 0 us
  other arithmetic: 96.2 us -> 2.37 us
  local copies, waits for them, and re-layouts: 37 us -> 10 us
  matrix products: 26.4 us -> 0 us
  starting transfers between devices: 20.1 us -> 0 us
  between operations: 17.2 us -> 0.66 us
    psum x2 -> x0, waiting for transfers between devices: 394 us -> none  [the longest x1 295 us: on_device(): grad_weight = lax.psum(replica_shard, 'dp')]
    reduce_scatter x1 -> x0, waiting for transfers between devices: 326 us -> none  [on_device(): lax.psum_scatter(jnp.dot(normed.T, d_proj, preferred_element_type=jnp.flo...]
    pallas_call x0 -> x3, Pallas kernels: none -> 214 us  [the longest x1 89.4 us: back(): pl.pallas_call(back_kernel, out_shape=(jax.ShapeDtypeStruct((ROWS, D), BF...]
    all_gather x1 -> x0, waiting for transfers between devices: 178 us -> none  [on_device(): lax.all_gather(w_glu, 'fsdp', axis=0, tiled=True)]
    psum x1 -> x0, blocking collectives: 78.8 us -> none  [on_device(): lax.psum((g_gain_in, g_kernel, g_gain_mid), ('dp', 'fsdp'))]
    reduce_sum x11 -> x0, other arithmetic: 60.3 us -> none  [the longest x6 31.1 us: kernel_grad(): jnp.sum(upstream * extended[j:j + width].astype(jnp.float32) * masks[:, j...]
    dot_general x3 -> x0, matrix products: 26.4 us -> none  [the longest x1 10.3 us: on_device(): jnp.dot(d_proj, lax.all_gather(w_glu, 'fsdp', axis=0, tiled=True).T, pref...]
    another operation x2 -> x0, other arithmetic: 24.8 us -> none
  transfers between devices with their start and end apart: 11 -> 0, of which waited for: 8 -> 0; matrix products, arithmetic and copies ran while one was open for 6% -> 0% of each run, Pallas kernels for 0% -> 0%
where the time goes in v1:
time: 227 us
  Pallas kernels  214 us (94%)
  local copies, waits for them, and re-layouts  10 us (4%)
  other arithmetic  2.37 us (1%)
    pallas_call x1, Pallas kernels, back(): pl.pallas_call(back_kernel, out_shape=(jax.ShapeDtypeStruct((ROWS, D), BF...  89.4 us
    pallas_call x1, Pallas kernels, front(): pl.pallas_call(front_kernel, out_shape=(jax.ShapeDtypeStruct((ROWS, D), B...  79.8 us
    pallas_call x1, Pallas kernels, middle(): pl.pallas_call(middle_kernel, out_shape=(jax.ShapeDtypeStruct((ROWS, D),...  44.8 us

profile of v1, /device:TPU:1, one launch (start us, length us, event | category | flops | bytes accessed | tf_op | source)
XLA Modules:
  0.0 227.0 jit_solution(1604372156269889205)
XLA Ops:
  0.6 1.2 reshape.23.dest
  1.9 0.7 reduce
  2.6 1.3 reshape.24.gain
  3.9 1.3 reshape.25.gain
  5.2 0.8 broadcast_in_dim.8.seg
  6.0 79.8 %front.1 = (bf16[384,1536]{1,0:T(8,128)(2,1)}, bf16[1536,384]{1,0:T(8,128)(2,1)}, bf16[1536,3072]{1,0:T(8,128)(2,1)}, f32[384,1536]{1,0:T(8,128)}, f32[384,1536]...) custom-call(bf16[384,1536]{1,0:T(8,128)(2,1)} %frames.1, ...), custom_call_target="tpu_custom_call" | custom-call | tf_op jit(solution)/shard_map/front/pallas_call | solution.py:210
  85.7 44.8 %middle.1 = (bf16[384,1536]{1,0:T(8,128)(2,1)}, bf16[2,384,1536]{2,1,0:T(8,128)(2,1)}, f32[32,1536]{1,0:T(8,128)}) custom-call(bf16[448,1536]{1,0:T(8,128)(2,1)} %get-tuple-element.20.gext, bf16[384,1536]{1,0:T(8,128)(2,1)} %get-tuple-element.21.packed, bf16[416,1536]{1,0:T(8,128)(2,1)} %get-tuple-element.22.cext, s32[448,128]{1,0:T(8,128)} %get-tuple-element.23.sext, ...), custom_call_target="tpu_custom_call" | custom-call | tf_op jit(solution)/shard_map/middle/pallas_call | solution.py:380
  130.5 89.4 %back.1 = (bf16[384,1536]{1,0:T(8,128)(2,1)}, bf16[2,192,1536]{2,1,0:T(8,128)(2,1)}, f32[40,1536]{1,0:T(8,128)}) custom-call(bf16[1536,384]{1,0:T(8,128)(2,1)} %get-tuple-element.27.normed_t, bf16[2,384,1536]{2,1,0:T(8,128)(2,1)} %get-tuple-element.28.d_proj, bf16[1536,3072]{1,0:T(8,128)(2,1)} %get-tuple-element.29.w, ...), custom_call_target="tpu_custom_call" | custom-call | tf_op jit(solution)/shard_map/back/pallas_call | solution.py:623
  219.9 1.5 slice_reduce_fusion
  221.3 1.6 slice.18
  223.0 1.3 slice_bitcast_fusion.1
  224.3 0.0 copy-start
  224.3 1.7 maximum_convert_fusion
  226.0 0.0 copy-done
  226.0 1.0 copy.15
Async XLA Ops:
  224.3 1.7 copy-start

commit v2 on v1

v2 whole, which is shorter than its diff:
```python
import jax
import jax.numpy as jnp
from jax import lax
from jax.experimental import pallas as pl
from jax.experimental.pallas import tpu as pltpu
from jax.sharding import PartitionSpec as P

EPS = 1e-05
ROWS = 384
D = 1536
TAPS = 31
MESH = pl.DeviceIdType.MESH
F32 = jnp.float32
BF16 = jnp.bfloat16
VMEM_LIMIT = 61 * 1024 * 1024


def place():
    dp = lax.axis_index("dp")
    me = lax.axis_index("fsdp")
    z_hi = lax.div(dp, 8)
    x = lax.rem(lax.div(dp, 2), 4)
    core = lax.rem(dp, 2)
    return dp, me, z_hi, x, core, lax.div(me, 2), lax.rem(me, 2)


def send(src, dst, send_sem, recv_sem, target):
    copy = pltpu.make_async_remote_copy(
        src_ref=src, dst_ref=dst, send_sem=send_sem, recv_sem=recv_sem, device_id=target, device_id_type=MESH
    )
    copy.start()
    return copy


def greet(targets):
    barrier = pltpu.get_barrier_semaphore()
    for target in targets:
        pl.semaphore_signal(barrier, inc=1, device_id=target, device_id_type=MESH)
    pl.semaphore_wait(barrier, len(targets))


def sigmoid(v):
    return 0.5 * jnp.tanh(0.5 * v) + 0.5


def vec_mean(v):
    return jnp.sum(v, axis=-1, keepdims=True) * (1.0 / D)


def block_kernel(
    frames, dest, segment, w, gain, cot, kern, gain_m,
    output, grad_frames, w_grad, small,
    packed, value, sig, gext, cext, sext, stat,
    w_all, out_buf, in_buf, normed, gx, mx, ex, kb, gk, seg, s1, s2,
    ncat, pcat, psend, dn, p0, p1, r0, r1, e0, e1, s0_in, s1_in, f, u_in, sa, sb, sy, sx, sz,
    a_s, a_r, y_s, y_r, z_s, z_r, b_s, b_r, h_s, h_r, l_s,
    c_s, c_r, q0_s, q0_r, q1_s, q1_r, m0_s, m0_r, m1_s, m1_r, u_s, u_r, v_s, v_r, x_s, x_r, d_s, d_r,
    k_s, k_r, ky_s, ky_r, kx_s, kx_r, kz_s, kz_r,
):
    dp, me, z_hi, x, core, y, z_lo = place()
    sib = (dp + 1 - 2 * core, me)
    up = (lax.rem(z_hi + z_lo, 4) * 8 + x * 2 + core, me + 1 - 2 * z_lo)
    down = (lax.rem(z_hi + 3 + z_lo, 4) * 8 + x * 2 + core, me + 1 - 2 * z_lo)
    far = (lax.rem(z_hi + 3 + 2 * z_lo, 4) * 8 + x * 2 + core, me + 1 - 2 * z_lo)
    nxt = (dp, lax.rem(me + 1, 8))
    prv = (dp, lax.rem(me + 7, 8))

    steps = (1, 3, 2)

    def x_of(s):
        return lax.rem(x + s, 4)

    def y_of(s):
        return lax.rem(y + s, 4)

    def z_of(s):
        return lax.rem(z_hi + s, 4)

    def x_dev(s):
        return (z_hi * 8 + x_of(s) * 2 + core, me)

    def y_dev(s):
        return (dp, 2 * y_of(s) + z_lo)

    def z_dev(s, same):
        return (z_of(s) * 8 + x * 2 + core, me if same else me + 1 - 2 * z_lo)

    pair = (dp, me + 1 - 2 * z_lo)
    greet(
        [(dp, lax.rem(me + s, 8)) for s in range(1, 8)]
        + [sib]
        + [x_dev(s) for s in steps]
        + [z_dev(s, True) for s in steps]
        + [z_dev(s, False) for s in steps]
    )
    sends = []

    half = core * 96
    y_copies = []
    for s in (1, 3, 2):
        peer = (dp, 2 * lax.rem(y + s, 4) + z_lo)
        y_copies.append(
            send(
                w.at[pl.ds(half, 96), :],
                w_all.at[pl.ds(192 * me + half, 96), :],
                y_s.at[s - 1], y_r.at[s - 1], peer,
            )
        )
    z_copies = [
        send(
            w.at[pl.ds(half + 48, 48), :], w_all.at[pl.ds(192 * me + half + 48, 48), :],
            z_s.at[0, 0], z_r.at[0, 0], up,
        ),
        send(
            w.at[pl.ds(half, 48), :], w_all.at[pl.ds(192 * me + half, 48), :],
            z_s.at[1, 0], z_r.at[1, 0], down,
        ),
    ]
    sext[32:416, :] = jnp.broadcast_to(segment[...].astype(F32), (128, ROWS)).T.astype(jnp.int32)
    halos = [
        send(cot.at[368:384, :], cext.at[0:16, :], h_s.at[0], h_r.at[0], nxt),
        send(cot.at[0:16, :], cext.at[400:416, :], h_s.at[1], h_r.at[1], prv),
        send(sext.at[384:416, :], sext.at[0:32, :], h_s.at[2], h_r.at[2], nxt),
        send(sext.at[32:64, :], sext.at[416:448, :], h_s.at[3], h_r.at[3], prv),
    ]
    cot_copy = pltpu.make_async_copy(cot, cext.at[16:400, :], l_s.at[0])
    cot_copy.start()

    d = dest[...].reshape(1, ROWS)
    gain_in = gain[...].reshape(1, D)
    k8 = lax.broadcasted_iota(jnp.int32, (8, ROWS), 0)
    rel = d - ROWS * k8
    hot = jnp.logical_and(rel >= 0, rel < ROWS)
    hot_f = jnp.where(hot, 1.0, 0.0).astype(F32)
    before = lax.broadcasted_iota(jnp.int32, (ROWS, ROWS), 0) < lax.broadcasted_iota(jnp.int32, (ROWS, ROWS), 1)
    rank = jnp.dot(hot_f.astype(BF16), jnp.where(before, 1.0, 0.0).astype(BF16), preferred_element_type=F32)
    order = jnp.sum(hot_f * (rank + 48.0 * k8.astype(F32)), axis=0, keepdims=True)
    slot = jnp.sum(hot_f * rel.astype(F32), axis=0, keepdims=True)
    high = jnp.floor(slot * (1.0 / 16.0))
    low = slot - 16.0 * high
    row_id = lax.broadcasted_iota(jnp.int32, (ROWS, ROWS), 0).astype(F32)
    perm = jnp.where(row_id == order, 1.0, 0.0).astype(BF16)
    tag_row = lax.broadcasted_iota(jnp.int32, (128, ROWS), 0)
    tags = jnp.where(tag_row == 0, high, jnp.where(tag_row == 1, low, 0.0)).astype(BF16)
    out_buf[:, D:] = lax.dot_general(perm, tags, (((1,), (1,)), ((), ())), preferred_element_type=F32).astype(BF16)
    for c in range(3):
        out_buf[:, 512 * c : 512 * c + 512] = jnp.dot(
            perm, frames[:, 512 * c : 512 * c + 512], preferred_element_type=F32
        ).astype(BF16)
    a_copies = []
    for s in (1, 7, 2, 6, 3, 5, 4):
        peer = lax.rem(me + s, 8)
        a_copies.append(
            send(
                out_buf.at[pl.ds(48 * peer, 48), :], in_buf.at[pl.ds(48 * me, 48), :],
                a_s.at[s - 1], a_r.at[s - 1], (dp, peer),
            )
        )
    own = pltpu.make_async_copy(out_buf.at[pl.ds(48 * me, 48), :], in_buf.at[pl.ds(48 * me, 48), :], l_s.at[1])
    own.start()
    own_w = pltpu.make_async_copy(w, w_all.at[pl.ds(192 * me, 192), :], l_s.at[2])
    own_w.start()

    b_copies = []

    def pass_on(shard, index):
        piece = w_all.at[pl.ds(192 * shard + half, 96), :]
        b_copies.append(send(piece, piece, b_s.at[index], b_r.at[index], sib))

    def y_arrived(n, s):
        y_copies[n].wait_recv()
        shard = 2 * lax.rem(y + 4 - s, 4) + z_lo
        base = 192 * shard + half
        top = w_all.at[pl.ds(base + 48, 48), :]
        low_rows = w_all.at[pl.ds(base, 48), :]
        z_copies.append(send(top, top, z_s.at[0, s], z_r.at[0, s], up))
        z_copies.append(send(low_rows, low_rows, z_s.at[1, s], z_r.at[1, s], down))
        pass_on(shard, s - 1)

    y_arrived(0, 1)
    y_arrived(1, 3)

    own.wait()
    for copy in a_copies:
        copy.wait_recv()
    tag = in_buf[:, D:].astype(F32)
    at = tag[:, 0:1] * 16.0 + tag[:, 1:2]
    col_id = lax.broadcasted_iota(jnp.int32, (ROWS, ROWS), 1).astype(F32)
    unperm = jnp.where(col_id == at, 1.0, 0.0).T.astype(BF16)
    for c in range(3):
        packed[:, 512 * c : 512 * c + 512] = jnp.dot(
            unperm, in_buf[:, 512 * c : 512 * c + 512], preferred_element_type=F32
        ).astype(BF16)

    def norm_body(i, carry):
        rows = pl.ds(pl.multiple_of(32 * i, 32), 32)
        v = packed[rows, :].astype(F32)
        mean = vec_mean(v)
        centre = v - mean
        scale = lax.rsqrt(vec_mean(centre * centre) + EPS)
        stat[0, rows, :] = jnp.broadcast_to(mean, (32, 128))
        stat[1, rows, :] = jnp.broadcast_to(scale, (32, 128))
        normed[rows, :] = (centre * scale * gain_in).astype(BF16)
        return carry

    lax.fori_loop(0, 12, norm_body, 0)
    for c in range(4):
        flipped = normed[:, 384 * c : 384 * c + 384].astype(F32).T.astype(BF16)
        for z in range(2):
            for p in range(2):
                to = 768 * p + 192 * c + 96 * z
                ncat[to : to + 96, 0:384] = flipped[192 * z + 96 * p : 192 * z + 96 * p + 96, :]

    share = send(ncat.at[:, 0:384], ncat.at[:, 384:768], c_s.at[0], c_r.at[0], sib)
    sends.append(share)
    y_arrived(2, 2)
    for n, t in enumerate((0, 1, 3, 2)):
        z_copies[2 * n].wait_recv()
        z_copies[2 * n + 1].wait_recv()
        pass_on(2 * lax.rem(y + 4 - t, 4) + 1 - z_lo, 3 + t)
    own_w.wait()
    for copy in b_copies:
        copy.wait_recv()

    def proj_body(i, carry):
        left = pl.ds(pl.multiple_of(256 * i, 256), 256)
        right = pl.ds(pl.multiple_of(256 * i + D, 256), 256)
        v = jnp.dot(normed[...], w_all[:, left], preferred_element_type=F32)
        g = jnp.dot(normed[...], w_all[:, right], preferred_element_type=F32)
        s = sigmoid(g)
        value[:, left] = v
        sig[:, left] = s
        gext[32:416, left] = (v * s).astype(BF16)
        return carry

    lax.fori_loop(0, 6, proj_body, 0)
    halos.append(send(gext.at[384:416, :], gext.at[0:32, :], h_s.at[4], h_r.at[4], nxt))
    halos.append(send(gext.at[32:64, :], gext.at[416:448, :], h_s.at[5], h_r.at[5], prv))

    for l in range(12):
        cols = slice(128 * l, 128 * l + 128)
        gx[l, 32:416, :] = gext[32:416, cols].astype(F32)
        for j in range(TAPS):
            kb[l, j] = jnp.broadcast_to(kern[j : j + 1, cols], (8, 128))
    gk[...] = jnp.zeros_like(gk)
    s1[...] = jnp.zeros_like(s1)
    cot_copy.wait()
    for copy in halos:
        copy.wait_recv()
    for l in range(12):
        cols = slice(128 * l, 128 * l + 128)
        gx[l, 0:32, :] = gext[0:32, cols].astype(F32)
        gx[l, 416:448, :] = gext[416:448, cols].astype(F32)
    edge = lax.broadcasted_iota(jnp.int32, (448, 128), 0) + ROWS * me - 32
    seg[...] = jnp.where(jnp.logical_and(edge >= 0, edge < 8 * ROWS), sext[...], -1)

    def conv_block(n, carry):
        base = pl.multiple_of(32 * lax.div(n, 4), 32)
        l0 = 3 * lax.rem(n, 4)
        total = [[jnp.zeros((8, 128), F32) for _ in range(4)] for _ in range(3)]
        here = [seg[pl.ds(base + 16 + 8 * t, 8), :] for t in range(4)]
        for j in range(TAPS):
            taps = [kb[l0 + i, j] for i in range(3)]
            for t in range(4):
                at = pl.ds(base + 1 + j + 8 * t, 8)
                same = seg[at, :] == here[t]
                for i in range(3):
                    total[i][t] = total[i][t] + jnp.where(same, gx[l0 + i, at, :], 0.0) * taps[i]
        for t in range(4):
            at = pl.ds(base + 8 * t, 8)
            for i in range(3):
                mx[l0 + i, at, :] = total[i][t]
            s1[at, :] += total[0][t] + total[1][t] + total[2][t]
        return carry

    lax.fori_loop(0, 52, conv_block, 0)

    def lane_mean(v):
        return jnp.broadcast_to(jnp.sum(v, axis=-1, keepdims=True) * (1.0 / D), v.shape)

    def stat_block(i, carry):
        rows = pl.ds(pl.multiple_of(104 * i, 8), 104)
        mean = lane_mean(s1[rows, :])
        square = jnp.zeros((104, 128), F32)
        for l in range(12):
            centre = mx[l, rows, :] - mean
            mx[l, rows, :] = centre
            square = square + centre * centre
        s1[rows, :] = lax.rsqrt(lane_mean(square) + EPS)
        return carry

    lax.fori_loop(0, 4, stat_block, 0)
    gain_mid = gain_m[...].reshape(1, D)

    def gate_rows(base, size, own, acc):
        rows = pl.ds(base, size)
        scale = s1[rows, :]
        sum_e = jnp.zeros((size, 128), F32)
        sum_eu = jnp.zeros((size, 128), F32)
        sums = []
        for l in range(12):
            cols = slice(128 * l, 128 * l + 128)
            unit = mx[l, rows, :] * scale
            mid = unit * gain_mid[:, cols]
            s = sigmoid(mid)
            gated = mid * s
            d_mid = cext[rows, cols].astype(F32) * (s + gated * (1.0 - s))
            if own:
                to = pl.ds(base - 16, size)
                output[to, cols] = (packed[to, cols].astype(F32) + gated).astype(BF16)
                du = d_mid * unit
                part = acc[l]
                for t in range(size // 8):
                    part = part + du[8 * t : 8 * t + 8, :]
                sums.append(part)
            e = d_mid * gain_mid[:, cols]
            sum_e = sum_e + e
            sum_eu = sum_eu + e * unit
            mx[l, rows, :] = unit
            ex[l, rows, :] = e
        s2[0, rows, :] = sum_e
        s2[1, rows, :] = sum_eu
        return tuple(sums)

    gate_rows(0, 16, False, None)
    gate_rows(400, 16, False, None)
    gain_acc = lax.fori_loop(
        0, 12, lambda i, acc: gate_rows(pl.multiple_of(16 + 32 * i, 16), 32, True, acc),
        tuple(jnp.zeros((8, 128), F32) for _ in range(12)),
    )

    def mixed_block(i, carry):
        rows = pl.ds(pl.multiple_of(104 * i, 8), 104)
        e_mean = lane_mean(s2[0, rows, :])
        eu_mean = lane_mean(s2[1, rows, :])
        scale = s1[rows, :]
        for l in range(12):
            mx[l, rows, :] = scale * (ex[l, rows, :] - e_mean - mx[l, rows, :] * eu_mean)
        return carry

    lax.fori_loop(0, 4, mixed_block, 0)

    stage0, stage1 = [], []
    own_half = pl.multiple_of(D * core, 128)
    other_half = pl.multiple_of(D - D * core, 128)
    for n, s in enumerate((1, 3, 2, 0)):
        q = x_of(s)
        q0 = pl.multiple_of(384 * q, 128)
        q_cols = pl.ds(q0, 384)
        l0 = 3 * q

        def back_block(b, carry, l0=l0, q0=q0):
            base = pl.multiple_of(32 * b, 32)
            total = [[jnp.zeros((8, 128), F32) for _ in range(4)] for _ in range(3)]
            glu = [[gx[l0 + i, pl.ds(base + 32 + 8 * t, 8), :] for t in range(4)] for i in range(3)]
            here = [seg[pl.ds(base + 32 + 8 * t, 8), :] for t in range(4)]
            for j in range(TAPS):
                taps = [kb[l0 + i, TAPS - 1 - j] for i in range(3)]
                grads = [None] * 3
                for t in range(4):
                    same = seg[pl.ds(base + 17 + j + 8 * t, 8), :] == here[t]
                    at = pl.ds(base + 1 + j + 8 * t, 8)
                    for i in range(3):
                        v = jnp.where(same, mx[l0 + i, at, :], 0.0)
                        total[i][t] = total[i][t] + v * taps[i]
                        grads[i] = glu[i][t] * v if t == 0 else grads[i] + glu[i][t] * v
                for i in range(3):
                    gk[l0 + i, TAPS - 1 - j] += grads[i]
            for i in range(3):
                cols = pl.ds(pl.multiple_of(q0 + 128 * i, 128), 128)
                for t in range(2):
                    rows = pl.ds(base + 16 * t, 16)
                    d_glu = jnp.concatenate([total[i][2 * t], total[i][2 * t + 1]], axis=0)
                    sg = sig[rows, cols]
                    d_value = d_glu * sg
                    d_gate = d_value * value[rows, cols] * (1.0 - sg)
                    pcat[rows, cols] = jnp.where(core == 0, d_value, d_gate).astype(BF16)
                    psend[rows, cols] = jnp.where(core == 0, d_gate, d_value).astype(BF16)
            return carry

        lax.fori_loop(0, 12, back_block, 0)
        swap = send(psend.at[:, q_cols], pcat.at[384:768, q_cols], d_s.at[n], d_r.at[n], sib)
        sends.append(swap)
        own_cols = pl.ds(pl.multiple_of(own_half + q0, 128), 384)
        other_cols = pl.ds(pl.multiple_of(other_half + q0, 128), 384)

        def dn_body(i, carry, n=n, q_cols=q_cols, own_cols=own_cols, other_cols=other_cols):
            cols = pl.ds(pl.multiple_of(256 * i, 256), 256)
            dims = (((1,), (1,)), ((), ()))
            part = lax.dot_general(
                pcat[0:384, q_cols], w_all[cols, own_cols], dims, preferred_element_type=F32
            ) + lax.dot_general(psend[:, q_cols], w_all[cols, other_cols], dims, preferred_element_type=F32)
            dn[:, cols] = part if n == 0 else dn[:, cols] + part
            return carry

        lax.fori_loop(0, 6, dn_body, 0)
        if n == 0:
            share.wait_recv()
        swap.wait_recv()

        def body0(i, carry, q_cols=q_cols):
            rows = pl.ds(pl.multiple_of(256 * i, 256), 256)
            p0[rows, q_cols] = jnp.dot(ncat[rows, :], pcat[:, q_cols], preferred_element_type=F32).astype(BF16)
            return carry

        def body1(i, carry, q=q, q_cols=q_cols):
            start = pl.multiple_of(256 * i, 256)
            p1[q, pl.ds(start, 256), :] = jnp.dot(
                ncat[pl.ds(768 + start, 256), :], pcat[:, q_cols], preferred_element_type=F32
            ).astype(BF16)
            return carry

        lax.fori_loop(0, 3, body1, 0)
        if s:
            stage1.append(send(p1.at[q], r1.at[s - 1], q1_s.at[s - 1], q1_r.at[s - 1], x_dev(s)))
        lax.fori_loop(0, 3, body0, 0)
        for k in steps:
            to = pl.ds(pl.multiple_of(192 * y_of(k), 64), 192)
            stage0.append(
                send(p0.at[to, q_cols], r0.at[k - 1, :, q_cols], q0_s.at[n, k - 1], q0_r.at[n, k - 1], y_dev(k))
            )
    sends += stage0 + stage1

    def frames_body(i, acc):
        base = pl.multiple_of(32 * i, 32)
        rows = pl.ds(base, 32)
        mean = stat[0, rows, :]
        scale = stat[1, rows, :]
        sum_e = jnp.zeros((32, 128), F32)
        sum_eu = jnp.zeros((32, 128), F32)
        sums = []
        for l in range(12):
            cols = slice(128 * l, 128 * l + 128)
            unit = (packed[rows, cols].astype(F32) - mean) * scale
            up = dn[rows, cols]
            du = up * unit
            sums.append(acc[l] + du[0:8] + du[8:16] + du[16:24] + du[24:32])
            e = up * gain_in[:, cols]
            sum_e = sum_e + e
            sum_eu = sum_eu + e * unit
        e_mean = lane_mean(sum_e)
        eu_mean = lane_mean(sum_eu)
        for l in range(12):
            cols = slice(128 * l, 128 * l + 128)
            unit = (packed[rows, cols].astype(F32) - mean) * scale
            e = dn[rows, cols] * gain_in[:, cols]
            grad_frames[rows, cols] = (
                cext[pl.ds(base + 16, 32), cols].astype(F32) + scale * (e - e_mean - unit * eu_mean)
            ).astype(BF16)
        return tuple(sums)

    in_acc = lax.fori_loop(0, 12, frames_body, tuple(jnp.zeros((8, 128), F32) for _ in range(12)))
    for l in range(12):
        cols = slice(128 * l, 128 * l + 128)
        for j in range(TAPS):
            sa[j : j + 1, cols] = jnp.sum(gk[l, j], axis=0, keepdims=True)
        sa[TAPS : TAPS + 1, cols] = jnp.sum(gain_acc[l], axis=0, keepdims=True)
        sa[32:40, cols] = jnp.broadcast_to(jnp.sum(in_acc[l], axis=0, keepdims=True), (8, 128))

    mine = pl.multiple_of(768 * core, 128)
    other = pl.multiple_of(768 - 768 * core, 128)
    small_a = send(sa.at[:, pl.ds(other, 768)], sb.at[:, 0:768], k_s.at[0], k_r.at[0], sib)

    for copy in stage0:
        copy.wait_recv()
    rows = pl.ds(pl.multiple_of(192 * y, 64), 192)
    for c in range(3):
        cols = slice(512 * c, 512 * c + 512)
        e0[:, cols] = (
            p0[rows, cols].astype(F32) + r0[0, :, cols].astype(F32) + r0[1, :, cols].astype(F32) + r0[2, :, cols].astype(F32)
        ).astype(BF16)
    second0 = [
        send(
            e0.at[:, pl.ds(pl.multiple_of(384 * x_of(s), 128), 384)], s0_in.at[s - 1],
            m0_s.at[s - 1], m0_r.at[s - 1], x_dev(s),
        )
        for s in steps
    ]
    small_a.wait_recv()
    sb[:, 768:1536] = sb[:, 0:768] + sa[:, pl.ds(mine, 768)]
    z_mine = pl.multiple_of(768 + 384 * z_lo, 128)
    z_other = pl.multiple_of(768 + 384 - 384 * z_lo, 128)
    small_b = send(sb.at[:, pl.ds(z_other, 384)], sy.at[4], k_s.at[1], k_r.at[1], pair)
    for copy in stage1:
        copy.wait_recv()
    for c in range(3):
        rows_c = slice(256 * c, 256 * c + 256)
        e1[rows_c, :] = (
            p1[x, rows_c, :].astype(F32) + r1[0, rows_c, :].astype(F32) + r1[1, rows_c, :].astype(F32) + r1[2, rows_c, :].astype(F32)
        ).astype(BF16)
    second1 = [
        send(
            e1.at[pl.ds(pl.multiple_of(192 * y_of(s), 64), 192), :], s1_in.at[s - 1],
            m1_s.at[s - 1], m1_r.at[s - 1], y_dev(s),
        )
        for s in steps
    ]
    small_b.wait_recv()
    sy[pl.ds(y, 1)] = (sb[:, pl.ds(z_mine, 384)] + sy[4])[None]
    y_small = [send(sy.at[y], sy.at[y], ky_s.at[s - 1], ky_r.at[s - 1], y_dev(s)) for s in steps]

    for copy in second0:
        copy.wait_recv()
    x_cols = pl.ds(pl.multiple_of(384 * x, 128), 384)
    sum0 = (
        e0[:, x_cols].astype(F32) + s0_in[0].astype(F32) + s0_in[1].astype(F32) + s0_in[2].astype(F32)
    ).astype(BF16)
    f[0, 0:96, :] = sum0[0:96, :]
    f[1, 0:96, :] = sum0[96:192, :]
    for copy in second1:
        copy.wait_recv()
    sum1 = (
        e1[rows, :].astype(F32) + s1_in[0].astype(F32) + s1_in[1].astype(F32) + s1_in[2].astype(F32)
    ).astype(BF16)
    f[0, 96:192, :] = sum1[0:96, :]
    f[1, 96:192, :] = sum1[96:192, :]
    third = []
    for s in (1, 3, 2, 0):
        for same in (False, True):
            if s or not same:
                n = 2 * s + (0 if same else 1)
                zb = z_lo if same else 1 - z_lo
                third.append(
                    send(
                        f.at[zb, pl.ds(pl.multiple_of(48 * z_of(s), 16), 48), :], u_in.at[n],
                        u_s.at[n], u_r.at[n], z_dev(s, same),
                    )
                )
    for copy in y_small:
        copy.wait_recv()
    sx[pl.ds(x, 1)] = (sy[0] + sy[1] + sy[2] + sy[3])[None]
    x_small = [send(sx.at[x], sx.at[x], kx_s.at[s - 1], kx_r.at[s - 1], x_dev(s)) for s in steps]
    for copy in third:
        copy.wait_recv()

    z_rows = pl.ds(pl.multiple_of(48 * z_hi, 16), 48)
    total = f[z_lo, z_rows, :].astype(F32)
    for n in range(1, 8):
        total = total + u_in[n].astype(F32)
    w_grad[pl.ds(core, 1), z_rows, x_cols] = total.astype(BF16)[None]
    piece = w_grad.at[core, z_rows, x_cols]
    fifth = [send(piece, piece, v_s.at[s - 1], v_r.at[s - 1], z_dev(s, True)) for s in steps]
    for copy in x_small:
        copy.wait_recv()
    sz[pl.ds(z_hi, 1)] = (sx[0] + sx[1] + sx[2] + sx[3])[None]
    z_small = [send(sz.at[z_hi], sz.at[z_hi], kz_s.at[s - 1], kz_r.at[s - 1], z_dev(s, True)) for s in steps]
    for copy in fifth:
        copy.wait_recv()
    strip = w_grad.at[core, :, x_cols]
    sixth = [send(strip, strip, x_s.at[s - 1], x_r.at[s - 1], x_dev(s)) for s in steps]
    seventh = [send(strip, strip, c_s.at[1], c_r.at[1], sib)]
    for copy in z_small:
        copy.wait_recv()
    col_here = pl.multiple_of(768 * core + 384 * z_lo, 128)
    small[:, pl.ds(col_here, 384)] = sz[0] + sz[1] + sz[2] + sz[3]
    here = small.at[:, pl.ds(col_here, 384)]
    small_z = send(here, here, k_s.at[2], k_r.at[2], pair)
    small_here = send(here, here, k_s.at[3], k_r.at[3], sib)
    for n, s in enumerate(steps):
        sixth[n].wait_recv()
        came = w_grad.at[core, :, pl.ds(pl.multiple_of(384 * x_of(4 - s), 128), 384)]
        seventh.append(send(came, came, c_s.at[1 + s], c_r.at[1 + s], sib))
    small_z.wait_recv()
    there = small.at[:, pl.ds(pl.multiple_of(768 * core + 384 - 384 * z_lo, 128), 384)]
    small_there = send(there, there, k_s.at[4], k_r.at[4], sib)
    small_here.wait_recv()
    small_there.wait_recv()
    for copy in seventh:
        copy.wait_recv()
    sends += [small_a, small_b, small_z, small_here, small_there]
    sends += y_small + x_small + z_small + second0 + second1 + third + fifth + sixth + seventh
    for copy in sends + halos + a_copies + y_copies + z_copies + b_copies:
        copy.wait_send()


def block(frames, dest, segment, w, gain, cot, kern, gain_m):
    vm = pl.BlockSpec(memory_space=pltpu.VMEM)
    hbm = pl.BlockSpec(memory_space=pl.ANY)
    sems = pltpu.SemaphoreType.DMA
    three = [sems((3,)), sems((3,))]
    return pl.pallas_call(
        block_kernel,
        out_shape=(
            jax.ShapeDtypeStruct((ROWS, D), BF16),
            jax.ShapeDtypeStruct((ROWS, D), BF16),
            jax.ShapeDtypeStruct((2, 192, D), BF16),
            jax.ShapeDtypeStruct((40, D), F32),
        ),
        in_specs=[vm, vm, vm, hbm, vm, hbm, vm, vm],
        out_specs=(vm, vm, vm, vm),
        scratch_shapes=[
            pltpu.VMEM((ROWS, D), BF16),
            pltpu.VMEM((ROWS, D), F32),
            pltpu.VMEM((ROWS, D), F32),
            pltpu.VMEM((448, D), BF16),
            pltpu.VMEM((416, D), BF16),
            pltpu.VMEM((448, 128), jnp.int32),
            pltpu.VMEM((2, ROWS, 128), F32),
            pltpu.VMEM((D, 2 * D), BF16),
            pltpu.VMEM((ROWS, D + 128), BF16),
            pltpu.VMEM((ROWS, D + 128), BF16),
            pltpu.VMEM((ROWS, D), BF16),
            pltpu.VMEM((12, 448, 128), F32),
            pltpu.VMEM((12, 416, 128), F32),
            pltpu.VMEM((12, 416, 128), F32),
            pltpu.VMEM((12, TAPS, 8, 128), F32),
            pltpu.VMEM((12, TAPS, 8, 128), F32),
            pltpu.VMEM((448, 128), jnp.int32),
            pltpu.VMEM((416, 128), F32),
            pltpu.VMEM((2, 416, 128), F32),
            pltpu.VMEM((D, 768), BF16),
            pltpu.VMEM((768, D), BF16),
            pltpu.VMEM((ROWS, D), BF16),
            pltpu.VMEM((ROWS, D), F32),
            pltpu.VMEM((768, D), BF16),
            pltpu.VMEM((4, 768, 384), BF16),
            pltpu.VMEM((3, 192, D), BF16),
            pltpu.VMEM((3, 768, 384), BF16),
            pltpu.VMEM((192, D), BF16),
            pltpu.VMEM((768, 384), BF16),
            pltpu.VMEM((3, 192, 384), BF16),
            pltpu.VMEM((3, 192, 384), BF16),
            pltpu.VMEM((2, 192, 384), BF16),
            pltpu.VMEM((8, 48, 384), BF16),
            pltpu.VMEM((40, D), F32),
            pltpu.VMEM((40, D), F32),
            pltpu.VMEM((5, 40, 384), F32),
            pltpu.VMEM((4, 40, 384), F32),
            pltpu.VMEM((4, 40, 384), F32),
            sems((7,)), sems((7,)),
            *three,
            sems((2, 4)), sems((2, 4)),
            sems((7,)), sems((7,)),
            sems((6,)), sems((6,)),
            sems((4,)),
            sems((5,)), sems((5,)),
            sems((4, 3)), sems((4, 3)),
            *three, *three, *three,
            sems((8,)), sems((8,)),
            *three, *three,
            sems((4,)), sems((4,)),
            sems((5,)), sems((5,)),
            *three, *three, *three,
        ],
        compiler_params=pltpu.CompilerParams(
            collective_id=0, has_side_effects=True, vmem_limit_bytes=VMEM_LIMIT
        ),
        name="block",
    )(frames, dest, segment, w, gain, cot, kern, gain_m)


def tail_kernel(w_grad, small, grad_weight, g_in, g_kernel, g_mid):
    for c in range(2):
        grad_weight[:, D * c : D * c + D] = w_grad[c].astype(F32)
    g_in[...] = small[32:33, :].reshape(D)
    g_kernel[...] = small[:TAPS, :]
    g_mid[...] = small[TAPS : TAPS + 1, :].reshape(D)


def tail(w_grad, small):
    vm = pl.BlockSpec(memory_space=pltpu.VMEM)
    return pl.pallas_call(
        tail_kernel,
        out_shape=(
            jax.ShapeDtypeStruct((192, 2 * D), F32),
            jax.ShapeDtypeStruct((D,), F32),
            jax.ShapeDtypeStruct((TAPS, D), F32),
            jax.ShapeDtypeStruct((D,), F32),
        ),
        in_specs=[vm] * 2,
        out_specs=(vm,) * 4,
        name="tail",
    )(w_grad, small)


def on_device(frames_in, dest, segment, gain_in, w_glu, kernel, gain_mid, cotangent):
    output, grad_frames, w_grad, small = block(
        frames_in, dest, segment, w_glu, gain_in, cotangent, kernel, gain_mid
    )
    return (output, grad_frames, *tail(w_grad, small))


def solution(mesh):
    return jax.shard_map(
        on_device,
        mesh=mesh,
        in_specs=(
            P(("dp", "fsdp"), None),
            P(("dp", "fsdp")),
            P("dp", "fsdp"),
            P(),
            P("fsdp", None),
            P(),
            P(),
            P(("dp", "fsdp"), None),
        ),
        out_specs=(
            P(("dp", "fsdp"), None),
            P(("dp", "fsdp"), None),
            P("fsdp", None),
            P(),
            P(),
            P(),
        ),
        check_vma=False,
    )
```

time: 227 us -> 182 us (0.80)
  Pallas kernels: 214 us -> 179 us
  local copies, waits for them, and re-layouts: 10 us -> 2.71 us
  other arithmetic: 2.37 us -> 0 us
    pallas_call x3 -> x2, Pallas kernels: 214 us -> 179 us  [the longest x1 176 us: block(): pl.pallas_call(block_kernel, out_shape=(jax.ShapeDtypeStruct((ROWS, D), B...]
    reshape x3 -> x0, local copies, waits for them, and re-layouts: 3.83 us -> none  [the longest x1 1.29 us: on_device(): gain = gain_in.reshape(1, D)]
    slice x2 -> x0, local copies, waits for them, and re-layouts: 3.07 us -> none  [the longest x1 1.62 us: on_device(): small[:TAPS]]
where the time goes in v2:
time: 182 us
  Pallas kernels  179 us (98%)
  local copies, waits for them, and re-layouts  2.71 us (1%)
    pallas_call x1, Pallas kernels, block(): pl.pallas_call(block_kernel, out_shape=(jax.ShapeDtypeStruct((ROWS, D), B...  176 us

profile of v2, /device:TPU:1, one launch (start us, length us, event | category | flops | bytes accessed | tf_op | source)
XLA Modules:
  0.0 182.3 jit_solution(7061468342447738959)
XLA Ops:
  0.6 175.9 %block.1 = (bf16[384,1536]{1,0:T(8,128)(2,1)}, bf16[384,1536]{1,0:T(8,128)(2,1)}, bf16[2,192,1536]{2,1,0:T(8,128)(2,1)}, f32[40,1536]{1,0:T(8,128)}) custom-call(bf16[384,1536]{1,0:T(8,128)(2,1)} %frames.1, s32[384]{0:T(512)} %dest.1, s32[1,384]{1,0:T(1,128)} %segment.1, bf16[192,3072]{1,0:T(8,128)(2,1)} %w.1, f32[1536]{0:T(1024)} %gain.1, ...), custom_call_target="tpu_custom_call" | custom-call | tf_op jit(solution)/shard_map/block/pallas_call | solution.py:581
  176.6 0.0 copy-start.1
  176.6 3.0 %tail.1 = (f32[192,3072]{1,0:T(8,128)}, f32[1536]{0:T(1024)}, f32[31,1536]{1,0:T(8,128)}, f32[1536]{0:T(1024)}) custom-call(bf16[2,192,1536]{2,1,0:T(8,128)(2,1)} %get-tuple-element.16.w_grad, f32[40,1536]{1,0:T(8,128)} %get-tuple-element.17.small), custom_call_target="tpu_custom_call" | custom-call | tf_op jit(solution)/shard_map/tail/pallas_call | solution.py:662
  179.6 0.0 copy-done.1
  179.6 0.0 copy-start
  179.6 1.0 copy.16
  180.6 0.7 copy-done
  181.3 1.0 copy.17
Async XLA Ops:
  176.6 3.0 %copy-start.1 = (bf16[384,1536]{1,0:T(8,128)(2,1)S(1)}, bf16[384,1536]{1,0:T(8,128)(2,1)}, u32[]{:S(2)}) copy-start(bf16[384,1536]{1,0:T(8,128)(2,1)} %get-tuple-element.28) | copy-start | bytes 3538948
  179.6 1.7 copy-start

commit v3 on v2

--- a/solution.py
+++ b/solution.py
@@ -51,9 +51,9 @@
     frames, dest, segment, w, gain, cot, kern, gain_m,
     output, grad_frames, w_grad, small,
     packed, value, sig, gext, cext, sext, stat,
-    w_all, out_buf, in_buf, normed, gx, mx, ex, kb, gk, seg, s1, s2,
+    w_all, out_buf, in_buf, normed, normed_k, gx, mx, ex, kb, gk, seg, s1, s2,
     ncat, pcat, psend, dn, p0, p1, r0, r1, e0, e1, s0_in, s1_in, f, u_in, sa, sb, sy, sx, sz,
-    a_s, a_r, y_s, y_r, z_s, z_r, b_s, b_r, h_s, h_r, l_s,
+    a_s, a_r, y_s, y_r, z_s, z_r, w_s, w_r, b_s, b_r, h_s, h_r, l_s,
     c_s, c_r, q0_s, q0_r, q1_s, q1_r, m0_s, m0_r, m1_s, m1_r, u_s, u_r, v_s, v_r, x_s, x_r, d_s, d_r,
     k_s, k_r, ky_s, ky_r, kx_s, kx_r, kz_s, kz_r,
 ):
@@ -96,25 +96,27 @@
     sends = []
 
     half = core * 96
+    par = lax.rem(x, 2)
+    c_mine = pl.multiple_of(D * par, 128)
+    c_else = pl.multiple_of(D - D * par, 128)
+    c_low = pl.ds(c_mine, 768)
+    c_high = pl.ds(pl.multiple_of(c_mine + 768, 128), 768)
+
+    def rows_of(shard):
+        return pl.ds(pl.multiple_of(192 * shard + half, 32), 96)
+
+    own_rows = pl.ds(pl.multiple_of(half, 32), 96)
     y_copies = []
-    for s in (1, 3, 2):
-        peer = (dp, 2 * lax.rem(y + s, 4) + z_lo)
+    for s in steps:
         y_copies.append(
             send(
-                w.at[pl.ds(half, 96), :],
-                w_all.at[pl.ds(192 * me + half, 96), :],
-                y_s.at[s - 1], y_r.at[s - 1], peer,
+                w.at[own_rows, pl.ds(c_mine, D)], w_all.at[rows_of(me), pl.ds(c_mine, D)],
+                y_s.at[s - 1], y_r.at[s - 1], y_dev(s),
             )
         )
     z_copies = [
-        send(
-            w.at[pl.ds(half + 48, 48), :], w_all.at[pl.ds(192 * me + half + 48, 48), :],
-            z_s.at[0, 0], z_r.at[0, 0], up,
-        ),
-        send(
-            w.at[pl.ds(half, 48), :], w_all.at[pl.ds(192 * me + half, 48), :],
-            z_s.at[1, 0], z_r.at[1, 0], down,
-        ),
+        send(w.at[own_rows, c_high], w_all.at[rows_of(me), c_high], z_s.at[0, 0], z_r.at[0, 0], up),
+        send(w.at[own_rows, c_low], w_all.at[rows_of(me), c_low], z_s.at[1, 0], z_r.at[1, 0], down),
     ]
     sext[32:416, :] = jnp.broadcast_to(segment[...].astype(F32), (128, ROWS)).T.astype(jnp.int32)
     halos = [
@@ -161,24 +163,45 @@
     own_w = pltpu.make_async_copy(w, w_all.at[pl.ds(192 * me, 192), :], l_s.at[2])
     own_w.start()
 
-    b_copies = []
+    b_copies, w_copies = {}, {}
+    shards = [2 * lax.rem(y + 4 - s, 4) + z_lo for s in steps]
+    shards += [2 * lax.rem(y + 4 - t, 4) + 1 - z_lo for t in (0,) + steps]
 
     def pass_on(shard, index):
-        piece = w_all.at[pl.ds(192 * shard + half, 96), :]
-        b_copies.append(send(piece, piece, b_s.at[index], b_r.at[index], sib))
+        rows = rows_of(shard)
+        high, low_piece = w_all.at[rows, c_high], w_all.at[rows, c_low]
+        w_copies[index] = [
+            send(high, high, w_s.at[0, index], w_r.at[0, index], x_dev(1)),
+            send(low_piece, low_piece, w_s.at[1, index], w_r.at[1, index], x_dev(3)),
+        ]
+        piece = w_all.at[rows, pl.ds(c_mine, D)]
+        b_copies[0, index] = send(piece, piece, b_s.at[0, index], b_r.at[0, index], sib)
 
     def y_arrived(n, s):
         y_copies[n].wait_recv()
-        shard = 2 * lax.rem(y + 4 - s, 4) + z_lo
-        base = 192 * shard + half
-        top = w_all.at[pl.ds(base + 48, 48), :]
-        low_rows = w_all.at[pl.ds(base, 48), :]
-        z_copies.append(send(top, top, z_s.at[0, s], z_r.at[0, s], up))
-        z_copies.append(send(low_rows, low_rows, z_s.at[1, s], z_r.at[1, s], down))
-        pass_on(shard, s - 1)
+        shard = shards[n]
+        rows = rows_of(shard)
+        high, low_piece = w_all.at[rows, c_high], w_all.at[rows, c_low]
+        z_copies.append(send(high, high, z_s.at[0, s], z_r.at[0, s], up))
+        z_copies.append(send(low_piece, low_piece, z_s.at[1, s], z_r.at[1, s], down))
+        pass_on(shard, n)
+
+    def z_arrived(n):
+        z_copies[2 * n].wait_recv()
+        z_copies[2 * n + 1].wait_recv()
+        pass_on(shards[3 + n], 3 + n)
+
+    def x_arrived(index):
+        for copy in w_copies[index]:
+            copy.wait_recv()
+        shard = shards[index]
+        piece = w_all.at[rows_of(shard), pl.ds(c_else, D)]
+        b_copies[1, index] = send(piece, piece, b_s.at[1, index], b_r.at[1, index], sib)
 
     y_arrived(0, 1)
     y_arrived(1, 3)
+    z_arrived(0)
+    y_arrived(2, 2)
 
     own.wait()
     for copy in a_copies:
@@ -192,6 +215,9 @@
             unperm, in_buf[:, 512 * c : 512 * c + 512], preferred_element_type=F32
         ).astype(BF16)
 
+    z_arrived(1)
+    z_arrived(2)
+
     def norm_body(i, carry):
         rows = pl.ds(pl.multiple_of(32 * i, 32), 32)
         v = packed[rows, :].astype(F32)
@@ -200,40 +226,63 @@
         scale = lax.rsqrt(vec_mean(centre * centre) + EPS)
         stat[0, rows, :] = jnp.broadcast_to(mean, (32, 128))
         stat[1, rows, :] = jnp.broadcast_to(scale, (32, 128))
-        normed[rows, :] = (centre * scale * gain_in).astype(BF16)
+        unit = (centre * scale * gain_in).astype(BF16)
+        normed[rows, :] = unit
+        for c in range(4):
+            for z in range(2):
+                at = 384 * c + 192 * z
+                normed_k[z, c, rows, :] = unit[:, at : at + 192]
         return carry
 
     lax.fori_loop(0, 12, norm_body, 0)
+    z_arrived(3)
+    for index in (0, 1, 3, 2):
+        x_arrived(index)
     for c in range(4):
         flipped = normed[:, 384 * c : 384 * c + 384].astype(F32).T.astype(BF16)
         for z in range(2):
             for p in range(2):
                 to = 768 * p + 192 * c + 96 * z
                 ncat[to : to + 96, 0:384] = flipped[192 * z + 96 * p : 192 * z + 96 * p + 96, :]
-
     share = send(ncat.at[:, 0:384], ncat.at[:, 384:768], c_s.at[0], c_r.at[0], sib)
     sends.append(share)
-    y_arrived(2, 2)
-    for n, t in enumerate((0, 1, 3, 2)):
-        z_copies[2 * n].wait_recv()
-        z_copies[2 * n + 1].wait_recv()
-        pass_on(2 * lax.rem(y + 4 - t, 4) + 1 - z_lo, 3 + t)
-    own_w.wait()
-    for copy in b_copies:
-        copy.wait_recv()
+    for index in (4, 5, 6):
+        x_arrived(index)
+
+    def proj(z, cols):
+        total = None
+        for c in range(4):
+            rows = pl.ds(pl.multiple_of(384 * c + 192 * z, 64), 192)
+            part = jnp.dot(normed_k[z, c], w_all[rows, cols], preferred_element_type=F32)
+            total = part if total is None else total + part
+        return total
 
     def proj_body(i, carry):
         left = pl.ds(pl.multiple_of(256 * i, 256), 256)
         right = pl.ds(pl.multiple_of(256 * i + D, 256), 256)
-        v = jnp.dot(normed[...], w_all[:, left], preferred_element_type=F32)
-        g = jnp.dot(normed[...], w_all[:, right], preferred_element_type=F32)
-        s = sigmoid(g)
+        value[:, left] = proj(z_lo, left)
+        sig[:, left] = proj(z_lo, right)
+        return carry
+
+    def proj_rest(i, carry):
+        left = pl.ds(pl.multiple_of(256 * i, 256), 256)
+        right = pl.ds(pl.multiple_of(256 * i + D, 256), 256)
+        v = value[:, left] + proj(1 - z_lo, left)
+        s = sigmoid(sig[:, left] + proj(1 - z_lo, right))
         value[:, left] = v
         sig[:, left] = s
         gext[32:416, left] = (v * s).astype(BF16)
         return carry
 
+    own_w.wait()
+    for index in (0, 1, 2):
+        b_copies[0, index].wait_recv()
+        b_copies[1, index].wait_recv()
     lax.fori_loop(0, 6, proj_body, 0)
+    for index in (3, 4, 5, 6):
+        b_copies[0, index].wait_recv()
+        b_copies[1, index].wait_recv()
+    lax.fori_loop(0, 6, proj_rest, 0)
     halos.append(send(gext.at[384:416, :], gext.at[0:32, :], h_s.at[4], h_r.at[4], nxt))
     halos.append(send(gext.at[32:64, :], gext.at[416:448, :], h_s.at[5], h_r.at[5], prv))
 
@@ -569,7 +618,9 @@
         copy.wait_recv()
     sends += [small_a, small_b, small_z, small_here, small_there]
     sends += y_small + x_small + z_small + second0 + second1 + third + fifth + sixth + seventh
-    for copy in sends + halos + a_copies + y_copies + z_copies + b_copies:
+    for pair_of in w_copies.values():
+        sends += pair_of
+    for copy in sends + halos + a_copies + y_copies + z_copies + list(b_copies.values()):
         copy.wait_send()
 
 
@@ -600,6 +651,7 @@
             pltpu.VMEM((ROWS, D + 128), BF16),
             pltpu.VMEM((ROWS, D + 128), BF16),
             pltpu.VMEM((ROWS, D), BF16),
+            pltpu.VMEM((2, 4, ROWS, 192), BF16),
             pltpu.VMEM((12, 448, 128), F32),
             pltpu.VMEM((12, 416, 128), F32),
             pltpu.VMEM((12, 416, 128), F32),
@@ -630,7 +682,8 @@
             sems((7,)), sems((7,)),
             *three,
             sems((2, 4)), sems((2, 4)),
-            sems((7,)), sems((7,)),
+            sems((2, 7)), sems((2, 7)),
+            sems((2, 7)), sems((2, 7)),
             sems((6,)), sems((6,)),
             sems((4,)),
             sems((5,)), sems((5,)),

time: 182 us -> 170 us (0.934)
  Pallas kernels: 179 us -> 167 us
    pallas_call x1, Pallas kernels: 176 us -> 164 us  [block(): pl.pallas_call(block_kernel, out_shape=(jax.ShapeDtypeStruct((ROWS, D), B...]
where the time goes in v3:
time: 170 us
  Pallas kernels  167 us (98%)
  local copies, waits for them, and re-layouts  2.71 us (2%)
    pallas_call x1, Pallas kernels, block(): pl.pallas_call(block_kernel, out_shape=(jax.ShapeDtypeStruct((ROWS, D), B...  164 us

profile of v3, /device:TPU:1, one launch (start us, length us, event | category | flops | bytes accessed | tf_op | source)
XLA Modules:
  0.0 170.0 jit_solution(9010756730967410462)
XLA Ops:
  0.6 163.6 %block.1 = (bf16[384,1536]{1,0:T(8,128)(2,1)}, bf16[384,1536]{1,0:T(8,128)(2,1)}, bf16[2,192,1536]{2,1,0:T(8,128)(2,1)}, f32[40,1536]{1,0:T(8,128)}) custom-call(bf16[384,1536]{1,0:T(8,128)(2,1)} %frames.1, s32[384]{0:T(512)} %dest.1, s32[1,384]{1,0:T(1,128)} %segment.1, bf16[192,3072]{1,0:T(8,128)(2,1)} %w.1, f32[1536]{0:T(1024)} %gain.1, ...), custom_call_target="tpu_custom_call" | custom-call | tf_op jit(solution)/shard_map/block/pallas_call | solution.py:632
  164.3 0.0 copy-start.1
  164.3 3.0 %tail.1 = (f32[192,3072]{1,0:T(8,128)}, f32[1536]{0:T(1024)}, f32[31,1536]{1,0:T(8,128)}, f32[1536]{0:T(1024)}) custom-call(bf16[2,192,1536]{2,1,0:T(8,128)(2,1)} %get-tuple-element.16.w_grad, f32[40,1536]{1,0:T(8,128)} %get-tuple-element.17.small), custom_call_target="tpu_custom_call" | custom-call | tf_op jit(solution)/shard_map/tail/pallas_call | solution.py:715
  167.3 0.0 copy-done.1
  167.3 0.0 copy-start
  167.3 1.0 copy.16
  168.3 0.7 copy-done
  169.0 1.0 copy.17
Async XLA Ops:
  164.3 3.0 %copy-start.1 = (bf16[384,1536]{1,0:T(8,128)(2,1)S(1)}, bf16[384,1536]{1,0:T(8,128)(2,1)}, u32[]{:S(2)}) copy-start(bf16[384,1536]{1,0:T(8,128)(2,1)} %get-tuple-element.28) | copy-start | bytes 3538948
  167.3 1.7 copy-start

commit v4 on v3

--- a/solution.py
+++ b/solution.py
@@ -51,8 +51,8 @@
     frames, dest, segment, w, gain, cot, kern, gain_m,
     output, grad_frames, w_grad, small,
     packed, value, sig, gext, cext, sext, stat,
-    w_all, out_buf, in_buf, normed, normed_k, gx, mx, ex, kb, gk, seg, s1, s2,
-    ncat, pcat, psend, dn, p0, p1, r0, r1, e0, e1, s0_in, s1_in, f, u_in, sa, sb, sy, sx, sz,
+    w_all, out_buf, in_buf, normed_k, gx, mx, ex, kb, gk, seg, s1, s2,
+    ncat, pcat, psend, dn, p0, p1, r0, r1, ry, rx, e0, e1, s0_in, s1_in, f, u_in, sa, sb, sy, sx, sz,
     a_s, a_r, y_s, y_r, z_s, z_r, w_s, w_r, b_s, b_r, h_s, h_r, l_s,
     c_s, c_r, q0_s, q0_r, q1_s, q1_r, m0_s, m0_r, m1_s, m1_r, u_s, u_r, v_s, v_r, x_s, x_r, d_s, d_r,
     k_s, k_r, ky_s, ky_r, kx_s, kx_r, kz_s, kz_r,
@@ -107,11 +107,11 @@
 
     own_rows = pl.ds(pl.multiple_of(half, 32), 96)
     y_copies = []
-    for s in steps:
+    for n, s in enumerate((1, 3)):
         y_copies.append(
             send(
                 w.at[own_rows, pl.ds(c_mine, D)], w_all.at[rows_of(me), pl.ds(c_mine, D)],
-                y_s.at[s - 1], y_r.at[s - 1], y_dev(s),
+                y_s.at[n], y_r.at[n], y_dev(s),
             )
         )
     z_copies = [
@@ -178,10 +178,16 @@
         b_copies[0, index] = send(piece, piece, b_s.at[0, index], b_r.at[0, index], sib)
 
     def y_arrived(n, s):
-        y_copies[n].wait_recv()
         shard = shards[n]
         rows = rows_of(shard)
         high, low_piece = w_all.at[rows, c_high], w_all.at[rows, c_low]
+        if n < 2:
+            y_copies[n].wait_recv()
+            piece = (low_piece, high)[n]
+            y_copies.append(send(piece, piece, y_s.at[2 + n], y_r.at[2 + n], y_dev(s)))
+        else:
+            y_copies[2].wait_recv()
+            y_copies[3].wait_recv()
         z_copies.append(send(high, high, z_s.at[0, s], z_r.at[0, s], up))
         z_copies.append(send(low_piece, low_piece, z_s.at[1, s], z_r.at[1, s], down))
         pass_on(shard, n)
@@ -227,7 +233,7 @@
         stat[0, rows, :] = jnp.broadcast_to(mean, (32, 128))
         stat[1, rows, :] = jnp.broadcast_to(scale, (32, 128))
         unit = (centre * scale * gain_in).astype(BF16)
-        normed[rows, :] = unit
+        psend[rows, :] = unit
         for c in range(4):
             for z in range(2):
                 at = 384 * c + 192 * z
@@ -239,7 +245,7 @@
     for index in (0, 1, 3, 2):
         x_arrived(index)
     for c in range(4):
-        flipped = normed[:, 384 * c : 384 * c + 384].astype(F32).T.astype(BF16)
+        flipped = psend[:, 384 * c : 384 * c + 384].astype(F32).T.astype(BF16)
         for z in range(2):
             for p in range(2):
                 to = 768 * p + 192 * c + 96 * z
@@ -389,10 +395,40 @@
 
     lax.fori_loop(0, 4, mixed_block, 0)
 
-    stage0, stage1 = [], []
+    relay0, stage0, relay1, stage1, second0 = [None] * 4, [None] * 4, [], [], []
+    turns = (2, 1, 3, 0)
+    y_rows = pl.ds(pl.multiple_of(192 * y, 64), 192)
+
+    def add_y(n):
+        for copy in stage0[n]:
+            copy.wait_recv()
+        s = turns[n]
+        cols = pl.ds(pl.multiple_of(384 * x_of(s), 128), 384)
+        e0[n] = (
+            p0[y_rows, cols].astype(F32)
+            + r0[0, :, cols].astype(F32)
+            + r0[1, :, cols].astype(F32)
+        ).astype(BF16)
+        if s:
+            second0.append(send(e0.at[n], s0_in.at[s - 1], m0_s.at[s - 1], m0_r.at[s - 1], x_dev(s)))
+
+    def far_y(k, offset, size):
+        return pl.ds(pl.multiple_of(192 * y_of(k) + offset, 32), size)
+
+    def relay_y(n):
+        cols = pl.ds(pl.multiple_of(384 * x_of(turns[n]), 128), 384)
+        for side, k, offset in ((0, 1, 0), (1, 3, 96)):
+            relay0[n][side].wait_recv()
+            rows = far_y(k, offset, 96)
+            p0[rows, cols] = (p0[rows, cols].astype(F32) + ry[side, :, cols].astype(F32)).astype(BF16)
+        stage0[n] = [
+            send(p0.at[far_y(k, 0, 192), cols], r0.at[side, :, cols], q0_s.at[n, 2 + side], q0_r.at[n, 2 + side], y_dev(k))
+            for side, k in ((0, 1), (1, 3))
+        ]
+
     own_half = pl.multiple_of(D * core, 128)
     other_half = pl.multiple_of(D - D * core, 128)
-    for n, s in enumerate((1, 3, 2, 0)):
+    for n, s in enumerate(turns):
         q = x_of(s)
         q0 = pl.multiple_of(384 * q, 128)
         q_cols = pl.ds(q0, 384)
@@ -430,45 +466,75 @@
         lax.fori_loop(0, 12, back_block, 0)
         swap = send(psend.at[:, q_cols], pcat.at[384:768, q_cols], d_s.at[n], d_r.at[n], sib)
         sends.append(swap)
-        own_cols = pl.ds(pl.multiple_of(own_half + q0, 128), 384)
-        other_cols = pl.ds(pl.multiple_of(other_half + q0, 128), 384)
-
-        def dn_body(i, carry, n=n, q_cols=q_cols, own_cols=own_cols, other_cols=other_cols):
-            cols = pl.ds(pl.multiple_of(256 * i, 256), 256)
-            dims = (((1,), (1,)), ((), ()))
-            part = lax.dot_general(
-                pcat[0:384, q_cols], w_all[cols, own_cols], dims, preferred_element_type=F32
-            ) + lax.dot_general(psend[:, q_cols], w_all[cols, other_cols], dims, preferred_element_type=F32)
-            dn[:, cols] = part if n == 0 else dn[:, cols] + part
-            return carry
-
-        lax.fori_loop(0, 6, dn_body, 0)
         if n == 0:
             share.wait_recv()
+        else:
+            relay_y(n - 1)
         swap.wait_recv()
 
         def body0(i, carry, q_cols=q_cols):
-            rows = pl.ds(pl.multiple_of(256 * i, 256), 256)
+            rows = pl.ds(pl.multiple_of(384 * i, 128), 384)
             p0[rows, q_cols] = jnp.dot(ncat[rows, :], pcat[:, q_cols], preferred_element_type=F32).astype(BF16)
             return carry
 
         def body1(i, carry, q=q, q_cols=q_cols):
-            start = pl.multiple_of(256 * i, 256)
-            p1[q, pl.ds(start, 256), :] = jnp.dot(
-                ncat[pl.ds(768 + start, 256), :], pcat[:, q_cols], preferred_element_type=F32
+            start = pl.multiple_of(384 * i, 128)
+            p1[q, pl.ds(start, 384), :] = jnp.dot(
+                ncat[pl.ds(768 + start, 384), :], pcat[:, q_cols], preferred_element_type=F32
             ).astype(BF16)
             return carry
 
-        lax.fori_loop(0, 3, body1, 0)
-        if s:
-            stage1.append(send(p1.at[q], r1.at[s - 1], q1_s.at[s - 1], q1_r.at[s - 1], x_dev(s)))
-        lax.fori_loop(0, 3, body0, 0)
-        for k in steps:
-            to = pl.ds(pl.multiple_of(192 * y_of(k), 64), 192)
-            stage0.append(
-                send(p0.at[to, q_cols], r0.at[k - 1, :, q_cols], q0_s.at[n, k - 1], q0_r.at[n, k - 1], y_dev(k))
-            )
-    sends += stage0 + stage1
+        lax.fori_loop(0, 2, body1, 0)
+        if s == 2:
+            relay1 = [
+                send(p1.at[q, 0:384, :], rx.at[0], q1_s.at[0], q1_r.at[0], x_dev(1)),
+                send(p1.at[q, 384:768, :], rx.at[1], q1_s.at[1], q1_r.at[1], x_dev(3)),
+            ]
+        elif s:
+            side = 0 if s == 1 else 1
+            relay1[side].wait_recv()
+            half_rows = slice(384 * side, 384 * side + 384)
+            p1[q, half_rows, :] = (p1[q, half_rows, :].astype(F32) + rx[side].astype(F32)).astype(BF16)
+            stage1.append(send(p1.at[q], r1.at[side], q1_s.at[2 + side], q1_r.at[2 + side], x_dev(s)))
+        lax.fori_loop(0, 2, body0, 0)
+        relay0[n] = [
+            send(p0.at[far_y(2, 96 * side, 96), q_cols], ry.at[side, :, q_cols], q0_s.at[n, side], q0_r.at[n, side], y_dev(k))
+            for side, k in ((0, 1), (1, 3))
+        ]
+        if n >= 2:
+            add_y(n - 2)
+
+    dims = (((1,), (1,)), ((), ()))
+
+    def dn_body(i, carry):
+        cols = pl.ds(pl.multiple_of(256 * i, 256), 256)
+        dn[:, cols] = lax.dot_general(
+            pcat[0:384, :], w_all[cols, pl.ds(own_half, D)], dims, preferred_element_type=F32
+        ) + lax.dot_general(psend[...], w_all[cols, pl.ds(other_half, D)], dims, preferred_element_type=F32)
+        return carry
+
+    lax.fori_loop(0, 3, dn_body, 0)
+    relay_y(3)
+    add_y(2)
+    lax.fori_loop(3, 6, dn_body, 0)
+    add_y(3)
+    for n in range(4):
+        sends += relay0[n] + stage0[n]
+    sends += relay1 + stage1
+    for copy in stage1:
+        copy.wait_recv()
+    for c in range(3):
+        rows_c = slice(256 * c, 256 * c + 256)
+        e1[rows_c, :] = (
+            p1[x, rows_c, :].astype(F32) + r1[0, rows_c, :].astype(F32) + r1[1, rows_c, :].astype(F32)
+        ).astype(BF16)
+    second1 = [
+        send(
+            e1.at[pl.ds(pl.multiple_of(192 * y_of(s), 64), 192), :], s1_in.at[s - 1],
+            m1_s.at[s - 1], m1_r.at[s - 1], y_dev(s),
+        )
+        for s in steps
+    ]
 
     def frames_body(i, acc):
         base = pl.multiple_of(32 * i, 32)
@@ -510,40 +576,11 @@
     other = pl.multiple_of(768 - 768 * core, 128)
     small_a = send(sa.at[:, pl.ds(other, 768)], sb.at[:, 0:768], k_s.at[0], k_r.at[0], sib)
 
-    for copy in stage0:
-        copy.wait_recv()
-    rows = pl.ds(pl.multiple_of(192 * y, 64), 192)
-    for c in range(3):
-        cols = slice(512 * c, 512 * c + 512)
-        e0[:, cols] = (
-            p0[rows, cols].astype(F32) + r0[0, :, cols].astype(F32) + r0[1, :, cols].astype(F32) + r0[2, :, cols].astype(F32)
-        ).astype(BF16)
-    second0 = [
-        send(
-            e0.at[:, pl.ds(pl.multiple_of(384 * x_of(s), 128), 384)], s0_in.at[s - 1],
-            m0_s.at[s - 1], m0_r.at[s - 1], x_dev(s),
-        )
-        for s in steps
-    ]
     small_a.wait_recv()
     sb[:, 768:1536] = sb[:, 0:768] + sa[:, pl.ds(mine, 768)]
     z_mine = pl.multiple_of(768 + 384 * z_lo, 128)
     z_other = pl.multiple_of(768 + 384 - 384 * z_lo, 128)
     small_b = send(sb.at[:, pl.ds(z_other, 384)], sy.at[4], k_s.at[1], k_r.at[1], pair)
-    for copy in stage1:
-        copy.wait_recv()
-    for c in range(3):
-        rows_c = slice(256 * c, 256 * c + 256)
-        e1[rows_c, :] = (
-            p1[x, rows_c, :].astype(F32) + r1[0, rows_c, :].astype(F32) + r1[1, rows_c, :].astype(F32) + r1[2, rows_c, :].astype(F32)
-        ).astype(BF16)
-    second1 = [
-        send(
-            e1.at[pl.ds(pl.multiple_of(192 * y_of(s), 64), 192), :], s1_in.at[s - 1],
-            m1_s.at[s - 1], m1_r.at[s - 1], y_dev(s),
-        )
-        for s in steps
-    ]
     small_b.wait_recv()
     sy[pl.ds(y, 1)] = (sb[:, pl.ds(z_mine, 384)] + sy[4])[None]
     y_small = [send(sy.at[y], sy.at[y], ky_s.at[s - 1], ky_r.at[s - 1], y_dev(s)) for s in steps]
@@ -552,14 +589,14 @@
         copy.wait_recv()
     x_cols = pl.ds(pl.multiple_of(384 * x, 128), 384)
     sum0 = (
-        e0[:, x_cols].astype(F32) + s0_in[0].astype(F32) + s0_in[1].astype(F32) + s0_in[2].astype(F32)
+        e0[3].astype(F32) + s0_in[0].astype(F32) + s0_in[1].astype(F32) + s0_in[2].astype(F32)
     ).astype(BF16)
     f[0, 0:96, :] = sum0[0:96, :]
     f[1, 0:96, :] = sum0[96:192, :]
     for copy in second1:
         copy.wait_recv()
     sum1 = (
-        e1[rows, :].astype(F32) + s1_in[0].astype(F32) + s1_in[1].astype(F32) + s1_in[2].astype(F32)
+        e1[y_rows, :].astype(F32) + s1_in[0].astype(F32) + s1_in[1].astype(F32) + s1_in[2].astype(F32)
     ).astype(BF16)
     f[0, 96:192, :] = sum1[0:96, :]
     f[1, 96:192, :] = sum1[96:192, :]
@@ -596,7 +633,7 @@
     for copy in fifth:
         copy.wait_recv()
     strip = w_grad.at[core, :, x_cols]
-    sixth = [send(strip, strip, x_s.at[s - 1], x_r.at[s - 1], x_dev(s)) for s in steps]
+    sixth = [send(strip, strip, x_s.at[n], x_r.at[n], x_dev(s)) for n, s in ((0, 1), (1, 3))]
     seventh = [send(strip, strip, c_s.at[1], c_r.at[1], sib)]
     for copy in z_small:
         copy.wait_recv()
@@ -605,13 +642,20 @@
     here = small.at[:, pl.ds(col_here, 384)]
     small_z = send(here, here, k_s.at[2], k_r.at[2], pair)
     small_here = send(here, here, k_s.at[3], k_r.at[3], sib)
-    for n, s in enumerate(steps):
+    for n, s in ((0, 1), (1, 3)):
         sixth[n].wait_recv()
-        came = w_grad.at[core, :, pl.ds(pl.multiple_of(384 * x_of(4 - s), 128), 384)]
-        seventh.append(send(came, came, c_s.at[1 + s], c_r.at[1 + s], sib))
+        came_cols = pl.ds(pl.multiple_of(384 * x_of(4 - s), 128), 384)
+        part = w_grad.at[core, 96 * n : 96 * n + 96, came_cols]
+        sixth.append(send(part, part, x_s.at[2 + n], x_r.at[2 + n], x_dev(s)))
+        came = w_grad.at[core, :, came_cols]
+        seventh.append(send(came, came, c_s.at[2 + n], c_r.at[2 + n], sib))
     small_z.wait_recv()
     there = small.at[:, pl.ds(pl.multiple_of(768 * core + 384 - 384 * z_lo, 128), 384)]
     small_there = send(there, there, k_s.at[4], k_r.at[4], sib)
+    sixth[2].wait_recv()
+    sixth[3].wait_recv()
+    came = w_grad.at[core, :, pl.ds(pl.multiple_of(384 * x_of(2), 128), 384)]
+    seventh.append(send(came, came, c_s.at[4], c_r.at[4], sib))
     small_here.wait_recv()
     small_there.wait_recv()
     for copy in seventh:
@@ -650,7 +694,6 @@
             pltpu.VMEM((D, 2 * D), BF16),
             pltpu.VMEM((ROWS, D + 128), BF16),
             pltpu.VMEM((ROWS, D + 128), BF16),
-            pltpu.VMEM((ROWS, D), BF16),
             pltpu.VMEM((2, 4, ROWS, 192), BF16),
             pltpu.VMEM((12, 448, 128), F32),
             pltpu.VMEM((12, 416, 128), F32),
@@ -666,9 +709,11 @@
             pltpu.VMEM((ROWS, D), F32),
             pltpu.VMEM((768, D), BF16),
             pltpu.VMEM((4, 768, 384), BF16),
-            pltpu.VMEM((3, 192, D), BF16),
-            pltpu.VMEM((3, 768, 384), BF16),
-            pltpu.VMEM((192, D), BF16),
+            pltpu.VMEM((2, 192, D), BF16),
+            pltpu.VMEM((2, 768, 384), BF16),
+            pltpu.VMEM((2, 96, D), BF16),
+            pltpu.VMEM((2, 384, 384), BF16),
+            pltpu.VMEM((4, 192, 384), BF16),
             pltpu.VMEM((768, 384), BF16),
             pltpu.VMEM((3, 192, 384), BF16),
             pltpu.VMEM((3, 192, 384), BF16),
@@ -680,17 +725,19 @@
             pltpu.VMEM((4, 40, 384), F32),
             pltpu.VMEM((4, 40, 384), F32),
             sems((7,)), sems((7,)),
-            *three,
+            sems((4,)), sems((4,)),
             sems((2, 4)), sems((2, 4)),
             sems((2, 7)), sems((2, 7)),
             sems((2, 7)), sems((2, 7)),
             sems((6,)), sems((6,)),
             sems((4,)),
             sems((5,)), sems((5,)),
-            sems((4, 3)), sems((4, 3)),
-            *three, *three, *three,
+            sems((4, 4)), sems((4, 4)),
+            sems((4,)), sems((4,)),
+            *three, *three,
             sems((8,)), sems((8,)),
-            *three, *three,
+            *three,
+            sems((4,)), sems((4,)),
             sems((4,)), sems((4,)),
             sems((5,)), sems((5,)),
             *three, *three, *three,
@@ -702,16 +749,25 @@
     )(frames, dest, segment, w, gain, cot, kern, gain_m)
 
 
-def tail_kernel(w_grad, small, grad_weight, g_in, g_kernel, g_mid):
+def tail_kernel(w_grad, small, out_in, frames_in, grad_weight, g_in, g_kernel, g_mid, output, grad_frames, sem):
+    copies = [
+        pltpu.make_async_copy(out_in, output, sem.at[0]),
+        pltpu.make_async_copy(frames_in, grad_frames, sem.at[1]),
+    ]
+    for copy in copies:
+        copy.start()
     for c in range(2):
         grad_weight[:, D * c : D * c + D] = w_grad[c].astype(F32)
     g_in[...] = small[32:33, :].reshape(D)
     g_kernel[...] = small[:TAPS, :]
     g_mid[...] = small[TAPS : TAPS + 1, :].reshape(D)
-
-
-def tail(w_grad, small):
+    for copy in copies:
+        copy.wait()
+
+
+def tail(w_grad, small, output, grad_frames):
     vm = pl.BlockSpec(memory_space=pltpu.VMEM)
+    hbm = pl.BlockSpec(memory_space=pl.ANY)
     return pl.pallas_call(
         tail_kernel,
         out_shape=(
@@ -719,18 +775,23 @@
             jax.ShapeDtypeStruct((D,), F32),
             jax.ShapeDtypeStruct((TAPS, D), F32),
             jax.ShapeDtypeStruct((D,), F32),
+            jax.ShapeDtypeStruct((ROWS, D), BF16),
+            jax.ShapeDtypeStruct((ROWS, D), BF16),
         ),
-        in_specs=[vm] * 2,
-        out_specs=(vm,) * 4,
+        in_specs=[vm] * 4,
+        out_specs=(vm, vm, vm, vm, hbm, hbm),
+        scratch_shapes=[pltpu.SemaphoreType.DMA((2,))],
+        compiler_params=pltpu.CompilerParams(vmem_limit_bytes=VMEM_LIMIT),
         name="tail",
-    )(w_grad, small)
+    )(w_grad, small, output, grad_frames)
 
 
 def on_device(frames_in, dest, segment, gain_in, w_glu, kernel, gain_mid, cotangent):
     output, grad_frames, w_grad, small = block(
         frames_in, dest, segment, w_glu, gain_in, cotangent, kernel, gain_mid
     )
-    return (output, grad_frames, *tail(w_grad, small))
+    grad_weight, g_in, g_kernel, g_mid, output, grad_frames = tail(w_grad, small, output, grad_frames)
+    return (output, grad_frames, grad_weight, g_in, g_kernel, g_mid)
 
 
 def solution(mesh):

time: 170 us -> 165 us (0.971)
  Pallas kernels: 167 us -> 164 us
  local copies, waits for them, and re-layouts: 2.71 us -> 0 us
    pallas_call x1, Pallas kernels: 164 us -> 159 us  [block(): pl.pallas_call(block_kernel, out_shape=(jax.ShapeDtypeStruct((ROWS, D), B...]
    unnamed x6 -> x0, local copies, waits for them, and re-layouts: 2.71 us -> none
    pallas_call x1, Pallas kernels: 3 us -> 5 us  [tail(): pl.pallas_call(tail_kernel, out_shape=(jax.ShapeDtypeStruct((192, 2 * D),...]
where the time goes in v4:
time: 165 us
  Pallas kernels  164 us (99%)
    pallas_call x1, Pallas kernels, block(): pl.pallas_call(block_kernel, out_shape=(jax.ShapeDtypeStruct((ROWS, D), B...  159 us
    pallas_call x1, Pallas kernels, tail(): pl.pallas_call(tail_kernel, out_shape=(jax.ShapeDtypeStruct((192, 2 * D),...  5 us

profile of v4, /device:TPU:1, one launch (start us, length us, event | category | flops | bytes accessed | tf_op | source)
XLA Modules:
  0.0 165.0 jit_solution(14105795972501374594)
XLA Ops:
  0.6 159.4 %block.1 = (bf16[384,1536]{1,0:T(8,128)(2,1)}, bf16[384,1536]{1,0:T(8,128)(2,1)}, bf16[2,192,1536]{2,1,0:T(8,128)(2,1)}, f32[40,1536]{1,0:T(8,128)}) custom-call(bf16[384,1536]{1,0:T(8,128)(2,1)} %frames.1, s32[384]{0:T(512)} %dest.1, s32[1,384]{1,0:T(1,128)} %segment.1, bf16[192,3072]{1,0:T(8,128)(2,1)} %w.1, f32[1536]{0:T(1024)} %gain.1, ...), custom_call_target="tpu_custom_call" | custom-call | tf_op jit(solution)/shard_map/block/pallas_call | solution.py:676
  160.0 5.0 %tail.1 = (f32[192,3072]{1,0:T(8,128)}, f32[1536]{0:T(1024)}, f32[31,1536]{1,0:T(8,128)}, f32[1536]{0:T(1024)}, bf16[384,1536]{1,0:T(8,128)(2,1)}, /*index=5*/bf16[384,1536]{1,0:T(8,128)(2,1)}) custom-call(bf16[2,192,1536]{2,1,0:T(8,128)(2,1)} %get-tuple-element.16.w_grad, f32[40,1536]{1,0:T(8,128)} %get-tuple-element.17.small, ...), custom_call_target="tpu_custom_call" | custom-call | tf_op jit(solution)/shard_map/tail/pallas_call | solution.py:771

commit v5 on v4

--- a/solution.py
+++ b/solution.py
@@ -48,9 +48,9 @@
 
 
 def block_kernel(
-    frames, dest, segment, w, gain, cot, kern, gain_m,
-    output, grad_frames, w_grad, small,
-    packed, value, sig, gext, cext, sext, stat,
+    frames_hbm, dest, segment, w, gain, cot, kern, gain_m,
+    output_hbm, grad_frames_hbm, w_grad, small,
+    frames, output, grad_frames, packed, value, sig, gext, cext, sext, stat,
     w_all, out_buf, in_buf, normed_k, gx, mx, ex, kb, gk, seg, s1, s2,
     ncat, pcat, psend, dn, p0, p1, r0, r1, ry, rx, e0, e1, s0_in, s1_in, f, u_in, sa, sb, sy, sx, sz,
     a_s, a_r, y_s, y_r, z_s, z_r, w_s, w_r, b_s, b_r, h_s, h_r, l_s,
@@ -86,6 +86,8 @@
         return (z_of(s) * 8 + x * 2 + core, me if same else me + 1 - 2 * z_lo)
 
     pair = (dp, me + 1 - 2 * z_lo)
+    frames_copy = pltpu.make_async_copy(frames_hbm, frames, l_s.at[3])
+    frames_copy.start()
     greet(
         [(dp, lax.rem(me + s, 8)) for s in range(1, 8)]
         + [sib]
@@ -145,6 +147,7 @@
     tag_row = lax.broadcasted_iota(jnp.int32, (128, ROWS), 0)
     tags = jnp.where(tag_row == 0, high, jnp.where(tag_row == 1, low, 0.0)).astype(BF16)
     out_buf[:, D:] = lax.dot_general(perm, tags, (((1,), (1,)), ((), ())), preferred_element_type=F32).astype(BF16)
+    frames_copy.wait()
     for c in range(3):
         out_buf[:, 512 * c : 512 * c + 512] = jnp.dot(
             perm, frames[:, 512 * c : 512 * c + 512], preferred_element_type=F32
@@ -384,6 +387,9 @@
         tuple(jnp.zeros((8, 128), F32) for _ in range(12)),
     )
 
+    output_copy = pltpu.make_async_copy(output, output_hbm, l_s.at[4])
+    output_copy.start()
+
     def mixed_block(i, carry):
         rows = pl.ds(pl.multiple_of(104 * i, 8), 104)
         e_mean = lane_mean(s2[0, rows, :])
@@ -565,6 +571,8 @@
         return tuple(sums)
 
     in_acc = lax.fori_loop(0, 12, frames_body, tuple(jnp.zeros((8, 128), F32) for _ in range(12)))
+    grad_frames_copy = pltpu.make_async_copy(grad_frames, grad_frames_hbm, l_s.at[5])
+    grad_frames_copy.start()
     for l in range(12):
         cols = slice(128 * l, 128 * l + 128)
         for j in range(TAPS):
@@ -662,6 +670,8 @@
         copy.wait_recv()
     sends += [small_a, small_b, small_z, small_here, small_there]
     sends += y_small + x_small + z_small + second0 + second1 + third + fifth + sixth + seventh
+    output_copy.wait()
+    grad_frames_copy.wait()
     for pair_of in w_copies.values():
         sends += pair_of
     for copy in sends + halos + a_copies + y_copies + z_copies + list(b_copies.values()):
@@ -681,9 +691,12 @@
             jax.ShapeDtypeStruct((2, 192, D), BF16),
             jax.ShapeDtypeStruct((40, D), F32),
         ),
-        in_specs=[vm, vm, vm, hbm, vm, hbm, vm, vm],
-        out_specs=(vm, vm, vm, vm),
+        in_specs=[hbm, vm, vm, hbm, vm, hbm, vm, vm],
+        out_specs=(hbm, hbm, vm, vm),
         scratch_shapes=[
+            pltpu.VMEM((ROWS, D), BF16),
+            pltpu.VMEM((ROWS, D), BF16),
+            pltpu.VMEM((ROWS, D), BF16),
             pltpu.VMEM((ROWS, D), BF16),
             pltpu.VMEM((ROWS, D), F32),
             pltpu.VMEM((ROWS, D), F32),
@@ -730,7 +743,7 @@
             sems((2, 7)), sems((2, 7)),
             sems((2, 7)), sems((2, 7)),
             sems((6,)), sems((6,)),
-            sems((4,)),
+            sems((6,)),
             sems((5,)), sems((5,)),
             sems((4, 4)), sems((4, 4)),
             sems((4,)), sems((4,)),

time: 165 us -> 164 us (level)
  no operation moved by 1% of the time
where the time goes in v5:
time: 164 us
  Pallas kernels  163 us (99%)
    pallas_call x1, Pallas kernels, block(): pl.pallas_call(block_kernel, out_shape=(jax.ShapeDtypeStruct((ROWS, D), B...  158 us
    pallas_call x1, Pallas kernels, tail(): pl.pallas_call(tail_kernel, out_shape=(jax.ShapeDtypeStruct((192, 2 * D),...  5 us

profile of v5, /device:TPU:1, one launch (start us, length us, event | category | flops | bytes accessed | tf_op | source)
XLA Modules:
  0.0 163.8 jit_solution(1590633839246206599)
XLA Ops:
  0.6 158.2 %block.1 = (bf16[384,1536]{1,0:T(8,128)(2,1)}, bf16[384,1536]{1,0:T(8,128)(2,1)}, bf16[2,192,1536]{2,1,0:T(8,128)(2,1)}, f32[40,1536]{1,0:T(8,128)}) custom-call(bf16[384,1536]{1,0:T(8,128)(2,1)} %frames_hbm.1, s32[384]{0:T(512)} %dest.1, s32[1,384]{1,0:T(1,128)} %segment.1, bf16[192,3072]{1,0:T(8,128)(2,1)} %w.1, f32[1536]{0:T(1024)} %gain.1, ...), custom_call_target="tpu_custom_call" | custom-call | tf_op jit(solution)/shard_map/block/pallas_call | solution.py:686
  158.8 5.0 %tail.1 = (f32[192,3072]{1,0:T(8,128)}, f32[1536]{0:T(1024)}, f32[31,1536]{1,0:T(8,128)}, f32[1536]{0:T(1024)}, bf16[384,1536]{1,0:T(8,128)(2,1)}, /*index=5*/bf16[384,1536]{1,0:T(8,128)(2,1)}) custom-call(bf16[2,192,1536]{2,1,0:T(8,128)(2,1)} %get-tuple-element.16.w_grad, f32[40,1536]{1,0:T(8,128)} %get-tuple-element.17.small, ...), custom_call_target="tpu_custom_call" | custom-call | tf_op jit(solution)/shard_map/tail/pallas_call | solution.py:784
